TPU v7x, 32 devices: a whole 2x2x4 slice. The times are simulated.
32 devices in a mesh: expert: 8 (over z, y), tensor: 4 (over x, core).
Axes of the slice: x: 2, y: 2, z: 4, core: 2. Of those that a mesh axis runs over, the one named last changes fastest.
Arguments:
- hidden_in: bfloat16 [4096, 1536], P('expert', 'tensor'), may hold values from -50 to 50
- cache_lengths: int32 [8], P('expert'), may hold values from 0 to 8192, as said below
- new_lengths: int32 [8], P('expert'), may hold values from 128 to 512, as said below
- key_cache: bfloat16 [8, 8192, 256], P('expert'), may hold values from -120 to 120
- cached_value_rows: bfloat16 [8, 8192, 256], P('expert'), may hold values from -6 to 6
- attn_gain: float32 [1536], replicated, may hold values from 0.1 to 1.9
- w_query: bfloat16 [1536, 1536], P(None, 'tensor'), may hold values from -0.15625 to 0.15625
- key_matrix: bfloat16 [1536, 256], replicated, may hold values from -0.15625 to 0.15625
- value_matrix: bfloat16 [1536, 256], replicated, may hold values from -0.15625 to 0.15625
- w_out: bfloat16 [1536, 1536], P('tensor'), may hold values from -0.5 to 0.5
- moe_gain: float32 [1536], replicated, may hold values from 0.1 to 1.9
- route_ids: int32 [4096, 4], P('expert'), may hold values from 0 to 7, all different within a row; in each aligned block of 512 rows (0 to 511, 512 to 1023, ...) at most 384 rows name the same one
- route_weights: float32 [4096, 4], P('expert'), may hold values from 0.1 to 1
- w_gate: bfloat16 [8, 1536, 768], P('expert', None, 'tensor'), may hold values from -0.15625 to 0.15625
- w_up: bfloat16 [8, 1536, 768], P('expert', None, 'tensor'), may hold values from -0.15625 to 0.15625
- w_down: bfloat16 [8, 768, 1536], P('expert', 'tensor'), may hold values from -0.21875 to 0.21875
Outputs:
- mixed: bfloat16 [4096, 1536], P('expert', 'tensor')
Inputs may be any that keep to these rules, and one draw needn't show every extreme that they name: `cache_lengths`: A third of the 8 requests, rounded up, hold an empty cache; at least one holds 8192 positions. `new_lengths`: at least one request has all 512 new tokens valid. `route_ids`: each row names 4 different experts. Within the 512 rows of one request no expert is named by more than 384 rows, and in some request some expert is named by exactly 384 rows.
All inputs are finite; a program needn't handle non-finite values.
Results may differ from a plain program's by a relative error of at most 0.013.
Values may be sent and summed in bfloat16 or wider, within the bound.
A program may use at most 192 MiB of HBM per device.

v0:
```python
import math

import jax
import jax.numpy as jnp
from jax import lax
from jax.sharding import PartitionSpec as P

QUERY_HEADS = 12
KEY_VALUE_HEADS = 2
HEAD_DIM = 128
TOP = 4


epsilon = 1e-06
contract = (((1,), (1,)), ((), ()))


def norm_rows(activity, gain_vector):
    values = activity.astype(jnp.float32)
    mean_square = jnp.mean(values * values, axis=-1, keepdims=True)
    return (values * lax.rsqrt(mean_square + epsilon) * gain_vector).astype(jnp.bfloat16)


def fresh_scores(query_rows, new_keys, new_length, scaling):
    scores = (
        lax.dot_general(query_rows, new_keys, contract, preferred_element_type=jnp.float32)
        * scaling
    )
    query_place = jnp.arange(query_rows.shape[0], dtype=jnp.int32)
    key_place = jnp.arange(new_keys.shape[0], dtype=jnp.int32)
    allowed = (key_place[None, :] <= query_place[:, None]) & (key_place[None, :] < new_length)
    return jnp.where(allowed, scores, -jnp.inf)


def attend_masked(
    query_rows, past_keys, past_values, cache_length, new_keys, new_values, new_length
):
    scaling = 1.0 / math.sqrt(query_rows.shape[1])
    cache_scores = (
        lax.dot_general(query_rows, past_keys, contract, preferred_element_type=jnp.float32)
        * scaling
    )
    cache_place = jnp.arange(past_keys.shape[0], dtype=jnp.int32)
    cache_scores = jnp.where(cache_place[None, :] < cache_length, cache_scores, -jnp.inf)
    new_scores = fresh_scores(query_rows, new_keys, new_length, scaling)
    row_max = jnp.maximum(jnp.max(cache_scores, axis=1), jnp.max(new_scores, axis=1))
    cache_weight = jnp.exp(cache_scores - row_max[:, None])
    new_weight = jnp.exp(new_scores - row_max[:, None])
    denominator = jnp.sum(cache_weight, axis=1) + jnp.sum(new_weight, axis=1)
    summed = jnp.dot(
        cache_weight.astype(jnp.bfloat16), past_values, preferred_element_type=jnp.float32
    )
    summed = summed + jnp.dot(
        new_weight.astype(jnp.bfloat16), new_values, preferred_element_type=jnp.float32
    )
    return (summed / denominator[:, None]).astype(jnp.bfloat16)


def slot_table(flat_ids, expert_total, capacity):
    one_hot = (flat_ids[:, None] == jnp.arange(expert_total, dtype=jnp.int32)[None, :]).astype(
        jnp.int32
    )
    earlier = jnp.cumsum(one_hot, axis=0) - one_hot
    slot_rank = jnp.sum(earlier * one_hot, axis=1)
    target_slot = flat_ids * capacity + slot_rank
    assignments = flat_ids.shape[0]
    owner_row = (
        jnp.full((expert_total * capacity,), -1, jnp.int32)
        .at[target_slot]
        .set(jnp.arange(assignments, dtype=jnp.int32) // TOP)
    )
    return (target_slot, owner_row)


def pack_rows(source_rows, owner_row, expert_total, capacity):
    filled = source_rows[jnp.maximum(owner_row, 0)]
    filled = jnp.where((owner_row >= 0)[:, None], filled, jnp.zeros((), jnp.bfloat16))
    return filled.reshape(expert_total, capacity, source_rows.shape[1])


def mix_rows(base_rows, returned, target_slot, weights_rows):
    width = returned.shape[-1]
    returned_rows = returned.reshape(-1, width)
    picked = returned_rows[target_slot].reshape(base_rows.shape[0], TOP, width)
    mixed_rows = base_rows.astype(jnp.float32)
    for slot_index in range(TOP):
        mixed_rows = mixed_rows + weights_rows[:, slot_index, None] * picked[:, slot_index].astype(
            jnp.float32
        )
    return mixed_rows.astype(jnp.bfloat16)


def local(
    hidden_in,
    cache_lengths,
    new_lengths,
    key_cache,
    cached_value_rows,
    attn_gain,
    w_query,
    key_matrix,
    value_matrix,
    w_out,
    moe_gain,
    route_ids,
    route_weights,
    w_gate,
    w_up,
    w_down,
):
    tensor_count = lax.axis_size("tensor")
    tensor_index = lax.axis_index("tensor")
    new_count = hidden_in.shape[0]
    slice_width = hidden_in.shape[1]
    model_width = slice_width * tensor_count
    local_heads = w_query.shape[1] // HEAD_DIM
    query_group_count = QUERY_HEADS // KEY_VALUE_HEADS
    shared = tensor_index * local_heads // query_group_count
    full_rows = lax.all_gather(hidden_in, "tensor", axis=1, tiled=True)
    attn_in = norm_rows(full_rows, attn_gain)
    queries = jnp.dot(attn_in, w_query, preferred_element_type=jnp.float32).astype(jnp.bfloat16)
    key_weight = lax.dynamic_slice_in_dim(key_matrix, shared * HEAD_DIM, HEAD_DIM, 1)
    value_weight = lax.dynamic_slice_in_dim(value_matrix, shared * HEAD_DIM, HEAD_DIM, 1)
    new_keys = jnp.dot(attn_in, key_weight, preferred_element_type=jnp.float32).astype(jnp.bfloat16)
    new_values = jnp.dot(attn_in, value_weight, preferred_element_type=jnp.float32).astype(
        jnp.bfloat16
    )
    past_keys = lax.dynamic_slice_in_dim(key_cache[0], shared * HEAD_DIM, HEAD_DIM, 1)
    past_values = lax.dynamic_slice_in_dim(cached_value_rows[0], shared * HEAD_DIM, HEAD_DIM, 1)
    cache_length = cache_lengths[0]
    new_length = new_lengths[0]
    heads_out = []
    for head_index in range(local_heads):
        query_part = queries[:, head_index * HEAD_DIM : (head_index + 1) * HEAD_DIM]
        heads_out.append(
            attend_masked(
                query_part, past_keys, past_values, cache_length, new_keys, new_values, new_length
            )
        )
    context = jnp.concatenate(heads_out, axis=1)
    partial_out = jnp.dot(context, w_out, preferred_element_type=jnp.float32)
    expert_total = w_gate.shape[0] * lax.axis_size("expert")
    capacity = 3 * TOP * new_count // (2 * expert_total)
    head_total = lax.psum(partial_out.astype(jnp.bfloat16), "tensor").astype(jnp.float32)
    residual = (full_rows.astype(jnp.float32) + head_total).astype(jnp.bfloat16)
    moe_rows = norm_rows(residual, moe_gain)
    residual_slice = lax.dynamic_slice_in_dim(residual, tensor_index * slice_width, slice_width, 1)
    target_slot, owner_row = slot_table(route_ids.reshape(-1), expert_total, capacity)
    received = lax.all_to_all(
        pack_rows(moe_rows, owner_row, expert_total, capacity),
        "expert",
        split_axis=0,
        concat_axis=0,
        tiled=True,
    )
    sources = received.shape[0]
    item_count = received.shape[1]
    flat_rows = received.reshape(sources * item_count, model_width)
    gate_value = jnp.dot(flat_rows, w_gate[0], preferred_element_type=jnp.float32)
    upward = jnp.dot(flat_rows, w_up[0], preferred_element_type=jnp.float32)
    active = (jnp.maximum(gate_value, 0.0) * upward).astype(jnp.bfloat16)
    partial_down = jnp.dot(active, w_down[0], preferred_element_type=jnp.float32).astype(
        jnp.bfloat16
    )
    expert_rows = (
        lax.psum_scatter(partial_down, "tensor", scatter_dimension=1, tiled=True)
        .astype(jnp.float32)
        .astype(jnp.bfloat16)
    )
    shaped = expert_rows.reshape(received.shape[0], received.shape[1], slice_width)
    returned = lax.all_to_all(shaped, "expert", split_axis=0, concat_axis=0, tiled=True)
    return mix_rows(residual_slice, returned, target_slot, route_weights)


def solution(mesh):
    placed = (
        P("expert", "tensor"),
        P("expert"),
        P("expert"),
        P("expert", None, None),
        P("expert", None, None),
        P(),
        P(None, "tensor"),
        P(),
        P(),
        P("tensor", None),
        P(),
        P("expert", None),
        P("expert", None),
        P("expert", None, "tensor"),
        P("expert", None, "tensor"),
        P("expert", "tensor", None),
    )
    return jax.shard_map(
        local, mesh=mesh, in_specs=placed, out_specs=P("expert", "tensor"), check_vma=False
    )
```

profile of v0, /device:TPU:1, one launch (start us, length us, event | category | flops | bytes accessed | tf_op | source)
XLA Modules:
  0.0 595.7 jit_solution(9840427401799433206)
XLA Ops:
  6.5 0.7 all-gather.2.cloned.1.call-update
  7.3 0.0 all-reduce.2.cloned.1.call-start
  7.3 0.8 copy.25
  8.2 0.2 eq.29
  8.3 0.2 eq.25
  9.8 2.3 reduce-window.6
  12.1 0.3 slice_reduce_fusion
  12.4 0.2 reduce-window.9
  12.6 0.7 broadcast_multiply_fusion
  13.3 0.1 copy.24
  13.4 0.2 mul.148
  13.7 0.1 add_bitcast_fusion
  13.8 17.3 %all-gather.2.cloned.1.call-done = bf16[512,1536]{1,0:T(8,128)(2,1)} async-done(((bf16[512,384]{1,0:T(8,128)(2,1)}), bf16[512,1536]{1,0:T(8,128)(2,1)}) %all-gather.2.cloned.1.call-update) | async-done | bytes 1572880 | tf_op jit(solution)/shard_map/all_gather | solution.py:119
  31.1 1.8 fusion.22
  32.9 0.0 copy-start.14
  32.9 0.0 copy-start.17
  32.9 2.9 convolution_convert_fusion.2
  35.8 0.0 copy-done.4
  35.9 0.0 copy-done.14
  35.9 0.0 copy-done.17
  35.9 0.0 copy-start.5
  35.9 0.6 convolution_convert_fusion.4
  36.5 1.3 fusion.115
  37.8 1.3 fusion.117
  39.1 1.3 fusion.116
  40.4 8.1 %fusion.29 = f32[512,8192]{1,0:T(8,128)} fusion(bf16[1,8192,256]{2,1,0:T(8,128)(2,1)S(1)} %copy-done.5, s32[]{:T(128)S(6)} %select_n.57, bf16[512,384]{1,0:T(8,128)(2,1)S(1)} %convolution_convert_fusion.2), kind=kOutput, calls=%fused_computation.45 | convolution fusion | flops 1073741824 | bytes 19005444 | tf_op jit(solution)/shard_map/dot_general | solution.py:40
  48.5 7.1 %fusion = (f32[512]{0:T(512)S(1)}, f32[512,8192]{1,0:T(8,128)}) fusion(pred[8192]{0:T(1024)(128)(4,1)S(1)} %iota_compare_fusion.3, bf16[1,8192,256]{2,1,0:T(8,128)(2,1)S(1)} %copy-done.5, s32[]{:T(128)S(6)} %select_n.57, bf16[512,384]{1,0:T(8,128)(2,1)S(1)} %convolution_convert_fusion.2), kind=kOutput, calls=%fused_computation.9 | convolution fusion | flops 1086324224 | bytes 19015684 | tf_op jit(solution)/shard_map/dot_general | solution.py:40
  55.6 19.2 %fusion.3 = (f32[512]{0:T(512)S(1)}, f32[512]{0:T(512)S(1)}, f32[512]{0:T(512)S(1)}, f32[512,8192]{1,0:T(8,128)}) fusion(f32[512,8192]{1,0:T(8,128)} %get-tuple-element.21, f32[512]{0:T(512)S(1)} %max.30, pred[8192]{0:T(1024)(128)(4,1)S(1)} %iota_compare_fusion.3, f32[512,8192]{1,0:T(8,128)} %fusion.29, bf16[1,8192,256]{2,1,0:T(8,128)(2,1)} %param.19, ...), kind=kOutput, calls=%fused_computation.12 | convolution fusion | flops 1115683328 | bytes 52576260 | tf_op jit(solution)/shard_map/dot_general | solution.py:40
  74.8 8.7 %fusion.13 = f32[512,128]{0,1:T(8,128)S(1)} fusion(f32[512,8192]{1,0:T(8,128)} %get-tuple-element.21, f32[512]{0:T(512)S(1)} %max.30, pred[8192]{0:T(1024)(128)(4,1)S(1)} %iota_compare_fusion.3, bf16[1,8192,256]{2,1,0:T(8,128)(2,1)} %param.20, s32[]{:T(128)S(6)} %select_n.57), kind=kOutput, calls=%fused_computation.22 | convolution fusion | flops 1090519040 | bytes 19146756 | tf_op jit(solution)/shard_map/dot_general | solution.py:50
  83.6 8.2 %fusion.11 = f32[512,128]{0,1:T(8,128)S(1)} fusion(f32[512,8192]{1,0:T(8,128)} %get-tuple-element.24, f32[512]{0:T(512)S(1)} %max.31, pred[8192]{0:T(1024)(128)(4,1)S(1)} %iota_compare_fusion.3, bf16[1,8192,256]{2,1,0:T(8,128)(2,1)S(1)} %copy-done.13, s32[]{:T(128)S(6)} %select_n.57), kind=kOutput, calls=%fused_computation.21 | convolution fusion | flops 1090519040 | bytes 19146756 | tf_op jit(solution)/shard_map/dot_general | solution.py:50
  91.8 13.6 %fusion.5 = (f32[512]{0:T(512)S(1)}, f32[512]{0:T(512)S(1)}) fusion(f32[512,8192]{1,0:T(8,128)} %get-tuple-element.24, f32[512]{0:T(512)S(1)} %max.31, pred[8192]{0:T(1024)(128)(4,1)S(1)} %iota_compare_fusion.3, f32[512]{0:T(512)S(1)} %max.32, f32[512,8192]{1,0:T(8,128)} %fusion.29), kind=kLoop, calls=%fused_computation.14 | loop fusion | flops 33553408 | bytes 33570816 | tf_op jit(solution)/shard_map/reduce_sum | solution.py:49
  105.5 0.0 copy-start.15
  105.5 8.2 %fusion.9 = f32[512,128]{0,1:T(8,128)S(1)} fusion(f32[512,8192]{1,0:T(8,128)} %fusion.29, f32[512]{0:T(512)S(1)} %max.32, pred[8192]{0:T(1024)(128)(4,1)S(1)} %iota_compare_fusion.3, bf16[1,8192,256]{2,1,0:T(8,128)(2,1)S(1)} %copy-done.13, s32[]{:T(128)S(6)} %select_n.57), kind=kOutput, calls=%fused_computation.20 | convolution fusion | flops 1090519040 | bytes 19146756 | tf_op jit(solution)/shard_map/dot_general | solution.py:50
  113.7 0.2 fusion.51
  113.9 0.2 fusion.53
  114.1 0.2 fusion.55
  114.3 0.6 convolution_convert_fusion.3
  115.0 0.3 fusion.49
  115.3 0.3 fusion.48
  115.6 0.3 fusion.47
  116.0 2.2 convolution_convert_fusion.1
  118.1 0.0 all-reduce.2.cloned.1.call-update
  118.2 0.0 reduce-scatter.4.cloned.1.call-start
  118.2 8.1 %scatter_custom_fusion = s32[3072]{0:T(1024)S(1)} fusion(s32[2048]{0:T(1024)S(1)} %bitcast.101, s32[2048]{0:T(1024)S(1)} %add_select_fusion, s32[]{:T(128)} %constant.60.clone.1), kind=kCustom, calls=%fused_computation.138 | custom fusion | bytes 12292 | tf_op jit(solution)/shard_map/scatter | solution.py:70
  126.4 34.3 %all-reduce.2.cloned.1.call-done = bf16[512,1536]{1,0:T(8,128)(2,1)} async-done(((bf16[512,1536]{1,0:T(8,128)(2,1)}), bf16[512,1536]{1,0:T(8,128)(2,1)}) %all-reduce.2.cloned.1.call-update) | async-done | bytes 1572880 | tf_op jit(solution)/shard_map/psum | solution.py:144
  160.6 2.0 fusion.19
  162.7 1.1 copy-done.3
  163.9 0.4 fusion.21
  164.3 14.9 %gather_fusion = bf16[3072,1536]{1,0:T(8,128)(2,1)} fusion(bf16[512,1536]{1,0:T(8,128)(2,1)S(1)} %fusion.21, s32[3072]{0:T(1024)S(1)} %maximum_clamp_fusion), kind=kCustom, calls=%fused_computation | custom fusion | bytes 18886656 | tf_op jit(solution)/shard_map/gather | solution.py:76
  179.2 8.1 %broadcast_select_fusion = bf16[8,384,1536]{2,1,0:T(8,128)(2,1)} fusion(bf16[8,384,1536]{2,1,0:T(8,128)(2,1)} %bitcast.95, pred[8,384]{1,0:T(8,128)(4,1)S(1)} %broadcast_in_dim.48), kind=kLoop, calls=%fused_computation.19 | loop fusion | flops 4718592 | bytes 18877440 | tf_op jit(solution)/shard_map/jit(_where)/select_n | solution.py:77
  187.3 210.0 %all_to_all.10 = bf16[8,384,1536]{2,1,0:T(8,128)(2,1)S(1)} all-to-all(bf16[8,384,1536]{2,1,0:T(8,128)(2,1)} %broadcast_select_fusion), channel_id=1, replica_groups=mesh['expert'=8,'tensor'=4] {'expert'}, dimensions={0} | all-to-all | bytes 18874368 | tf_op jit(solution)/shard_map/all_to_all | solution.py:149
  397.3 3.7 copy-done.2
  401.0 3.2 convolution_maximum_fusion
  404.2 14.9 %convolution_convert_fusion = bf16[3072,1536]{1,0:T(8,128)(2,1)} fusion(f32[3072,192]{0,1:T(8,128)S(1)} %convolution_maximum_fusion, bf16[3072,1536]{1,0:T(8,128)(2,1)} %bitcast.97, bf16[1,192,1536]{2,1,0:T(8,128)(2,1)S(1)} %copy-done.9, bf16[1,1536,192]{1,2,0:T(8,128)(2,1)S(1)} %copy-done.10), kind=kOutput, calls=%fused_computation.18 | convolution fusion | flops 3629776896 | bytes 22413312 | tf_op jit(solution)/shard_map/dot_general | solution.py:162
  419.1 12.7 %copy.31 = bf16[3072,1536]{0,1:T(8,128)(2,1)} copy(bf16[3072,1536]{1,0:T(8,128)(2,1)} %convolution_convert_fusion) | data formatting | bytes 18874368
  431.8 0.0 reduce-scatter.4.cloned.1.call-update
  431.8 78.1 %reduce-scatter.4.cloned.1.call-done = bf16[384,3072]{1,0:T(8,128)(2,1)} async-done(((bf16[1536,3072]{1,0:T(8,128)(2,1)}), bf16[384,3072]{1,0:T(8,128)(2,1)}) %reduce-scatter.4.cloned.1.call-update) | async-done | bytes 2359312
  509.9 4.3 copy.32
  514.2 5.2 all-to-all-start.1
  519.5 53.0 %all-to-all-done.1 = bf16[8,384,384]{2,1,0:T(8,128)(2,1)S(1)} async-done(((bf16[8,384,384]{2,1,0:T(8,128)(2,1)}), bf16[8,384,384]{2,1,0:T(8,128)(2,1)S(1)}, u32[]{:S(2)}, u32[]{:S(2)}) %all-to-all-start.1) | async-done | bytes 2359328 | tf_op jit(solution)/shard_map/all_to_all | solution.py:171
  572.5 9.0 %gather_fusion.1 = bf16[2048,384]{1,0:T(8,128)(2,1)} fusion(bf16[3072,384]{1,0:T(8,128)(2,1)S(1)} %bitcast.93, s32[2048]{0:T(1024)S(1)} %broadcast_clamp_fusion), kind=kCustom, calls=%fused_computation.1 | custom fusion | bytes 3153920 | tf_op jit(solution)/shard_map/gather | solution.py:84
  581.5 3.0 reshape.138
  584.5 2.3 fusion.113
  586.8 2.3 fusion.58
  (47 shorter events, 0.2 us)
Async XLA Ops:
  6.5 109.4 %copy-start = (bf16[384,1536]{1,0:T(8,128)(2,1)S(1)}, bf16[384,1536]{1,0:T(8,128)(2,1)}, u32[]{:S(2)}) copy-start(bf16[384,1536]{1,0:T(8,128)(2,1)} %param.25) | copy-start | bytes 3538948
  6.5 24.5 %all-gather.2.cloned.1.call-start = ((), (), s32[]{:S(2)}) async-start(), calls=%async_computation.3 | async-start | bytes 1966080 | tf_op jit(solution)/shard_map/all_gather | solution.py:119
  7.3 153.4 %all-reduce.2.cloned.1.call-start = ((), (), s32[]{:S(2)}) async-start(), calls=%async_computation.4 | async-start | bytes 3145728 | tf_op jit(solution)/shard_map/psum | solution.py:144
  32.9 3.0 copy-start.4
  32.9 3.0 copy-start.14
  32.9 3.0 copy-start.17
  35.9 4.5 copy-start.5
  74.8 8.8 %copy-start.13 = (bf16[1,8192,256]{2,1,0:T(8,128)(2,1)S(1)}, bf16[1,8192,256]{2,1,0:T(8,128)(2,1)}, u32[]{:S(2)}) copy-start(bf16[1,8192,256]{2,1,0:T(8,128)(2,1)} %param.20) | copy-start | bytes 12582916
  105.5 8.2 %copy-start.8 = (f32[512,512]{0,1:T(8,128)S(1)}, f32[512,512]{0,1:T(8,128)}, u32[]{:S(2)}) copy-start(f32[512,512]{0,1:T(8,128)} %get-tuple-element.23) | copy-start | bytes 3145732
  105.5 8.4 %copy-start.7 = (f32[512,512]{0,1:T(8,128)S(1)}, f32[512,512]{0,1:T(8,128)}, u32[]{:S(2)}) copy-start(f32[512,512]{0,1:T(8,128)} %get-tuple-element.28) | copy-start | bytes 3145732
  105.5 8.6 %copy-start.6 = (f32[512,512]{0,1:T(8,128)S(1)}, f32[512,512]{0,1:T(8,128)}, u32[]{:S(2)}) copy-start(f32[512,512]{0,1:T(8,128)} %get-tuple-element.26) | copy-start | bytes 3145732
  105.5 8.8 %copy-start.15 = (bf16[1536,256]{1,0:T(8,128)(2,1)S(1)}, bf16[1536,256]{1,0:T(8,128)(2,1)}, u32[]{:S(2)}) copy-start(bf16[1536,256]{1,0:T(8,128)(2,1)} %param.24) | copy-start | bytes 2359300
  118.1 45.7 %copy-start.11 = (f32[1536]{0:T(1024)S(1)}, f32[1536]{0:T(1024)}, u32[]{:S(2)}) copy-start(f32[1536]{0:T(1024)} %param.26) | copy-start | bytes 18436
  118.2 391.8 %reduce-scatter.4.cloned.1.call-start = ((), (), s32[]{:S(2)}) async-start(), calls=%async_computation.5 | async-start | bytes 11796480
  162.7 1.2 copy-start.3
  187.3 213.7 %copy-start.16 = (bf16[1,1536,192]{1,2,0:T(8,128)(2,1)S(1)}, bf16[1,1536,192]{1,2,0:T(8,128)(2,1)}, u32[]{:S(2)}) copy-start(bf16[1,1536,192]{1,2,0:T(8,128)(2,1)} %param.29) | copy-start | bytes 1769476
  397.3 3.7 copy-start.2
  401.0 3.2 copy-start.9
  401.0 3.2 copy-start.10
  509.9 9.5 %copy-start.12 = (f32[512,4]{0,1:T(4,128)S(1)}, f32[512,4]{0,1:T(4,128)}, u32[]{:S(2)}) copy-start(f32[512,4]{0,1:T(4,128)} %param.28) | copy-start | bytes 24580
  514.2 58.2 %all-to-all-start.1 = ((bf16[8,384,384]{2,1,0:T(8,128)(2,1)}), bf16[8,384,384]{2,1,0:T(8,128)(2,1)S(1)}, u32[]{:S(2)}, u32[]{:S(2)}) async-start(bf16[8,384,384]{2,1,0:T(8,128)(2,1)} %bitcast.98), calls=%async_computation.1 | async-start | bytes 4718592 | tf_op jit(solution)/shard_map/all_to_all | solution.py:171
  581.5 7.6 %copy-start.1 = (bf16[384,1536]{1,0:T(8,128)(2,1)S(1)}, bf16[384,1536]{1,0:T(8,128)(2,1)}, u32[]{:S(2)}) copy-start(bf16[384,1536]{1,0:T(8,128)(2,1)} %param.25) | copy-start | bytes 3538948
Sparse Core Ops, SparseCore 0:
  8.9 22.1 all-gather.1
  118.3 42.3 all-reduce.1
  431.9 77.9 reduce-scatter.3
where the time goes:
time: 598 us; the launch traced here: 596 us
  blocking collectives  210 us (35%)
  waiting for transfers between devices  183 us (31%)
  matrix products  88.8 us (15%)
  local copies, waits for them, and re-layouts  61 us (10%)
  other arithmetic  32.2 us (5%)
  between operations  14.9 us (2%)
    all_to_all x1, blocking collectives, local(): lax.all_to_all(pack_rows(moe_rows, owner_row, expert_total, capacity), 'e...  210 us
    unnamed x4, waiting for transfers between devices  78.9 us
    all_to_all x1, waiting for transfers between devices, local(): lax.all_to_all(shaped, 'expert', split_axis=0, concat_axis=0, tiled=True)  53 us
    dot_general x3, matrix products, attend_masked(): lax.dot_general(query_rows, past_keys, contract, preferred_element_type=j...  34.4 us
    psum x1, waiting for transfers between devices, local(): lax.psum(partial_out.astype(jnp.bfloat16), 'tensor').astype(jnp.float32)  34.3 us
    dot_general x3, matrix products, attend_masked(): jnp.dot(cache_weight.astype(jnp.bfloat16), past_values, preferred_element...  25.1 us
    unnamed x39, local copies, waits for them, and re-layouts  22.7 us
    all_gather x1, waiting for transfers between devices, local(): full_rows = lax.all_gather(hidden_in, 'tensor', axis=1, tiled=True)  17.3 us
  transfers between devices with their start and end apart: 4, of which 4 were waited for; matrix products, arithmetic and copies ran while one was open for 2% of the time, Pallas kernels for 0%

commit v1 on v0

v1 whole, which is shorter than its diff:
```python
import functools
import math

import jax
import jax.numpy as jnp
from jax import lax
from jax.experimental import pallas as pl
from jax.experimental.pallas import tpu as pltpu
from jax.sharding import PartitionSpec as P

QUERY_HEADS = 12
KEY_VALUE_HEADS = 2
HEAD_DIM = 128
TOP = 4
BLOCK = 1024

epsilon = 1e-06


def norm_rows(activity, gain_vector):
    values = activity.astype(jnp.float32)
    mean_square = jnp.mean(values * values, axis=-1, keepdims=True)
    return (values * lax.rsqrt(mean_square + epsilon) * gain_vector).astype(jnp.bfloat16)


def attention_kernel(
    heads, scale, info, q_ref, nk_ref, nv_ref, k_ref, v_ref, out_ref, top, total, acc
):
    step = pl.program_id(0)
    length = info[0]
    fresh = info[1]
    block = k_ref.shape[1]
    rows = q_ref.shape[1]

    def visit(head, keys, values, mask, first):
        scores = jnp.dot(
            keys,
            q_ref[head * HEAD_DIM : (head + 1) * HEAD_DIM, :],
            preferred_element_type=jnp.float32,
        )
        if mask is not None:
            scores = jnp.where(mask, scores, -jnp.inf)
        largest = jnp.max(scores, axis=0, keepdims=True)
        if not first:
            before = top[head : head + 1, :]
            largest = jnp.maximum(largest, before)
        weights = jnp.exp2((scores - largest) * scale)
        added = jnp.sum(weights, axis=0, keepdims=True)
        product = lax.dot_general(
            values,
            weights.astype(jnp.bfloat16),
            (((0,), (0,)), ((), ())),
            preferred_element_type=jnp.float32,
        )
        if not first:
            alpha = jnp.exp2((before - largest) * scale)
            added = added + total[head : head + 1, :] * alpha
            product = product + acc[head] * alpha
        top[head : head + 1, :] = largest
        total[head : head + 1, :] = added
        acc[head] = product

    @pl.when(step == 0)
    def _():
        count = nk_ref.shape[0]
        key_place = lax.broadcasted_iota(jnp.int32, (count, rows), 0)
        query_place = lax.broadcasted_iota(jnp.int32, (count, rows), 1)
        mask = (key_place <= query_place) & (key_place < fresh)
        for head in range(heads):
            visit(head, nk_ref[...], nv_ref[...], mask, True)

    start = (step - 1) * block

    @pl.when((step > 0) & (start + block <= length))
    def _():
        for head in range(heads):
            visit(head, k_ref[0], v_ref[0], None, False)

    @pl.when((step > 0) & (start < length) & (start + block > length))
    def _():
        place = lax.broadcasted_iota(jnp.int32, (block, rows), 0) + start
        for head in range(heads):
            visit(head, k_ref[0], v_ref[0], place < length, False)

    @pl.when(step == pl.num_programs(0) - 1)
    def _():
        for head in range(heads):
            result = acc[head] / total[head : head + 1, :]
            out_ref[:, head * HEAD_DIM : (head + 1) * HEAD_DIM] = result.T.astype(jnp.bfloat16)


def attention(queries_t, new_keys, new_values, keys, values, length, fresh, shared):
    heads = queries_t.shape[0] // HEAD_DIM
    rows = queries_t.shape[1]
    limit = keys.shape[1]
    block = min(BLOCK, limit)
    scale = math.log2(math.e) / math.sqrt(HEAD_DIM)
    info = jnp.stack([length, fresh, shared]).astype(jnp.int32)

    def place(step, info):
        last = jnp.maximum((info[0] + block - 1) // block - 1, 0)
        return (0, jnp.minimum(jnp.maximum(step - 1, 0), last), info[2])

    return pl.pallas_call(
        functools.partial(attention_kernel, heads, scale),
        grid_spec=pltpu.PrefetchScalarGridSpec(
            num_scalar_prefetch=1,
            grid=(1 + limit // block,),
            in_specs=[
                pl.BlockSpec(queries_t.shape, lambda step, info: (0, 0)),
                pl.BlockSpec(new_keys.shape, lambda step, info: (0, 0)),
                pl.BlockSpec(new_values.shape, lambda step, info: (0, 0)),
                pl.BlockSpec((1, block, HEAD_DIM), place),
                pl.BlockSpec((1, block, HEAD_DIM), place),
            ],
            out_specs=pl.BlockSpec((rows, heads * HEAD_DIM), lambda step, info: (0, 0)),
            scratch_shapes=[
                pltpu.VMEM((8, rows), jnp.float32),
                pltpu.VMEM((8, rows), jnp.float32),
                pltpu.VMEM((heads, HEAD_DIM, rows), jnp.float32),
            ],
        ),
        out_shape=jax.ShapeDtypeStruct((rows, heads * HEAD_DIM), jnp.bfloat16),
        compiler_params=pltpu.CompilerParams(vmem_limit_bytes=40 * 1024 * 1024),
        cost_estimate=pl.CostEstimate(
            flops=4 * heads * rows * limit * HEAD_DIM,
            bytes_accessed=4 * limit * HEAD_DIM,
            transcendentals=heads * rows * limit,
        ),
        name="attention",
    )(info, queries_t, new_keys, new_values, keys, values)


def local(
    hidden_in,
    cache_lengths,
    new_lengths,
    key_cache,
    cached_value_rows,
    attn_gain,
    w_query,
    key_matrix,
    value_matrix,
    w_out,
    moe_gain,
    route_ids,
    route_weights,
    w_gate,
    w_up,
    w_down,
):
    tensor_count = lax.axis_size("tensor")
    tensor_index = lax.axis_index("tensor")
    expert_index = lax.axis_index("expert")
    new_count = hidden_in.shape[0]
    quarter = new_count // tensor_count
    local_heads = w_query.shape[1] // HEAD_DIM
    query_group_count = QUERY_HEADS // KEY_VALUE_HEADS
    shared = tensor_index * local_heads // query_group_count
    expert_total = w_gate.shape[0] * lax.axis_size("expert")

    full_rows = lax.all_gather(hidden_in, "tensor", axis=1, tiled=True)
    whole_out = lax.all_gather(w_out, "tensor", axis=0, tiled=True)
    whole_gate = lax.all_gather(w_gate[0], "tensor", axis=0, tiled=False)
    whole_up = lax.all_gather(w_up[0], "tensor", axis=0, tiled=False)
    whole_down = lax.all_gather(w_down[0], "tensor", axis=0, tiled=True)

    my_ids = lax.dynamic_slice_in_dim(route_ids, tensor_index * quarter, quarter, 0)
    my_weights = lax.dynamic_slice_in_dim(route_weights, tensor_index * quarter, quarter, 0)
    named = my_ids[:, :, None] == jnp.arange(expert_total, dtype=jnp.int32)[None, None, :]
    table = jnp.sum(jnp.where(named, my_weights[:, :, None], 0.0), axis=1)
    tables = lax.all_gather(table, "expert", axis=0, tiled=True)
    row_weight = lax.dynamic_slice_in_dim(tables, expert_index, 1, 1)

    attn_in = norm_rows(full_rows, attn_gain)
    queries_t = lax.dot_general(
        w_query, attn_in, (((0,), (1,)), ((), ())), preferred_element_type=jnp.float32
    ).astype(jnp.bfloat16)
    key_weight = lax.dynamic_slice_in_dim(key_matrix, shared * HEAD_DIM, HEAD_DIM, 1)
    value_weight = lax.dynamic_slice_in_dim(value_matrix, shared * HEAD_DIM, HEAD_DIM, 1)
    both = jnp.dot(
        attn_in,
        jnp.concatenate([key_weight, value_weight], axis=1),
        preferred_element_type=jnp.float32,
    ).astype(jnp.bfloat16)
    context = attention(
        queries_t,
        both[:, :HEAD_DIM],
        both[:, HEAD_DIM:],
        key_cache,
        cached_value_rows,
        cache_lengths[0],
        new_lengths[0],
        shared,
    )
    my_context = lax.all_to_all(context, "tensor", split_axis=0, concat_axis=1, tiled=True)
    my_rows = lax.dynamic_slice_in_dim(full_rows, tensor_index * quarter, quarter, 0)
    residual = (
        my_rows.astype(jnp.float32)
        + jnp.dot(my_context, whole_out, preferred_element_type=jnp.float32)
    ).astype(jnp.bfloat16)
    moe_rows = norm_rows(residual, moe_gain)
    all_rows = lax.all_gather(moe_rows, "expert", axis=0, tiled=True)
    partial = jnp.zeros((all_rows.shape[0], all_rows.shape[1]), jnp.float32)
    actives = []
    for part in range(tensor_count):
        gate_value = jnp.dot(all_rows, whole_gate[part], preferred_element_type=jnp.float32)
        upward = jnp.dot(all_rows, whole_up[part], preferred_element_type=jnp.float32)
        actives.append((jnp.maximum(gate_value, 0.0) * upward).astype(jnp.bfloat16))
    active = jnp.concatenate(actives, axis=1)
    partial = jnp.dot(active, whole_down, preferred_element_type=jnp.float32)
    weighted = jnp.where(row_weight > 0.0, partial * row_weight, 0.0).astype(jnp.bfloat16)
    summed = lax.psum_scatter(weighted, "expert", scatter_dimension=0, tiled=True)
    mixed = (residual.astype(jnp.float32) + summed.astype(jnp.float32)).astype(jnp.bfloat16)
    return lax.all_to_all(mixed, "tensor", split_axis=1, concat_axis=0, tiled=True)


def solution(mesh):
    placed = (
        P("expert", "tensor"),
        P("expert"),
        P("expert"),
        P("expert", None, None),
        P("expert", None, None),
        P(),
        P(None, "tensor"),
        P(),
        P(),
        P("tensor", None),
        P(),
        P("expert", None),
        P("expert", None),
        P("expert", None, "tensor"),
        P("expert", None, "tensor"),
        P("expert", "tensor", None),
    )
    return jax.shard_map(
        local, mesh=mesh, in_specs=placed, out_specs=P("expert", "tensor"), check_vma=False
    )
```

time: 598 us -> 312 us (0.52)
  blocking collectives: 210 us -> 34.5 us
  matrix products: 88.8 us -> 31.5 us
  local copies, waits for them, and re-layouts: 61 us -> 6.51 us
  other arithmetic: 32.2 us -> 3.86 us
  Pallas kernels: 0 us -> 26.8 us
    all_to_all x1, blocking collectives: 210 us -> 10.3 us  [local(): lax.all_to_all(mixed, 'tensor', split_axis=1, concat_axis=0, tiled=True)]
    all_gather x0 -> x5, waiting for transfers between devices: none -> 85.9 us  [the longest x1 53.8 us: local(): all_rows = lax.all_gather(moe_rows, 'expert', axis=0, tiled=True)]
    unnamed x4 -> x7, waiting for transfers between devices: 78.9 us -> 3.18 us
    reduce_scatter x0 -> x1, waiting for transfers between devices: none -> 73.3 us  [local(): lax.psum_scatter(weighted, 'expert', scatter_dimension=0, tiled=True)]
    dot_general x18 -> x12, matrix products: 88.8 us -> 31.5 us  [the longest x4 10.1 us: local(): jnp.dot(all_rows, whole_up[part], preferred_element_type=jnp.float32)]
    all_to_all x1, waiting for transfers between devices: 53 us -> 6.68 us  [local(): lax.all_to_all(context, 'tensor', split_axis=0, concat_axis=1, tiled=True)]
    psum x1 -> x0, waiting for transfers between devices: 34.3 us -> none  [local(): lax.psum(partial_out.astype(jnp.bfloat16), 'tensor').astype(jnp.float32)]
    pallas_call x0 -> x1, Pallas kernels: none -> 26.8 us  [attention(): pl.pallas_call(functools.partial(attention_kernel, heads, scale), grid_sp...]
  transfers between devices with their start and end apart: 4 -> 8, of which waited for: 4 -> 6; matrix products, arithmetic and copies ran while one was open for 2% -> 10% of each run, Pallas kernels for 0% -> 9%
where the time goes in v1:
time: 312 us; the launch traced here: 311 us
  waiting for transfers between devices  188 us (60%)
  blocking collectives  34.5 us (11%)
  matrix products  31.5 us (10%)
  Pallas kernels  26.8 us (9%)
  between operations  15 us (5%)
  local copies, waits for them, and re-layouts  6.51 us (2%)
  starting transfers between devices  4.54 us (1%)
  other arithmetic  3.86 us (1%)
    reduce_scatter x1, waiting for transfers between devices, local(): lax.psum_scatter(weighted, 'expert', scatter_dimension=0, tiled=True)  73.3 us
    all_gather x1, waiting for transfers between devices, local(): all_rows = lax.all_gather(moe_rows, 'expert', axis=0, tiled=True)  53.8 us
    pallas_call x1, Pallas kernels, attention(): pl.pallas_call(functools.partial(attention_kernel, heads, scale), grid_sp...  26.8 us
    all_gather x1, blocking collectives, local(): tables = lax.all_gather(table, 'expert', axis=0, tiled=True)  24.2 us
    all_gather x1, waiting for transfers between devices, local(): full_rows = lax.all_gather(hidden_in, 'tensor', axis=1, tiled=True)  19 us
    all_gather x1, waiting for transfers between devices, local(): whole_up = lax.all_gather(w_up[0], 'tensor', axis=0, tiled=False)  16.7 us
    all_gather x1, waiting for transfers between devices, local(): whole_down = lax.all_gather(w_down[0], 'tensor', axis=0, tiled=True)  15.4 us
    all_to_all x1, blocking collectives, local(): lax.all_to_all(mixed, 'tensor', split_axis=1, concat_axis=0, tiled=True)  10.3 us
  transfers between devices with their start and end apart: 8, of which 6 were waited for; matrix products, arithmetic and copies ran while one was open for 10% of the time, Pallas kernels for 9%

profile of v1, /device:TPU:1, one launch (start us, length us, event | category | flops | bytes accessed | tf_op | source)
XLA Modules:
  0.0 310.9 jit_solution(2034861696234277166)
XLA Ops:
  6.5 0.0 copy-start
  6.5 0.0 copy-start.9
  6.5 0.0 all-gather.8.cloned.1.call-start
  6.5 0.7 all-gather.8.cloned.1.call-update
  7.3 0.0 all-gather.10.cloned.1.call-start
  7.3 0.7 all-gather.10.cloned.1.call-update
  8.0 0.0 all-gather.14.cloned.1.call-start
  8.1 0.7 all-gather.14.cloned.1.call-update
  10.1 0.1 pad_add_fusion.info
  10.1 1.9 constant_dynamic-slice_fusion.3
  12.0 19.0 %all-gather.8.cloned.1.call-done = bf16[512,1536]{1,0:T(8,128)(2,1)} async-done(((bf16[512,384]{1,0:T(8,128)(2,1)}), bf16[512,1536]{1,0:T(8,128)(2,1)}) %all-gather.8.cloned.1.call-update) | async-done | bytes 1572880 | tf_op jit(solution)/shard_map/all_gather | solution.py:162
  31.1 1.8 fusion
  32.9 0.0 copy-start.3
  32.9 0.0 copy-done.9
  32.9 0.0 copy-start.2
  32.9 2.3 convolution_convert_fusion.1
  35.2 0.0 copy-start.1
  35.2 0.0 copy-done
  35.2 0.0 copy-done.3
  35.2 0.9 fusion.17.q_ref
  36.2 0.0 copy-done.2
  36.2 1.4 copy-done.1
  37.6 26.8 %attention.1 = bf16[512,384]{1,0:T(8,128)(2,1)S(1)} custom-call(s32[3]{0:T(128)S(1)} %pad_add_fusion.info, bf16[384,512]{1,0:T(8,128)(2,1)S(1)} %fusion.17.q_ref, bf16[512,128]{1,0:T(8,128)(2,1)S(1)} %get-tuple-element.8.nk_ref, bf16[512,128]{1,0:T(8,128)(2,1)S(1)} %get-tuple-element.7.nv_ref, bf16[1,8192,256]{2,1,0:T(8,128)(2,1)S(1)} %copy-done.1, ...), custom_call_target="tpu_custom_call" | custom-call | flops 6442450944 | bytes 4194304 | tf_op jit(solution)/shard_map/attention/pallas_call | solution.py:104
  64.4 0.9 copy.32
  65.3 4.3 %all-to-all-start = ((bf16[4,128,384]{1,2,0:T(8,128)(2,1)}), bf16[4,128,384]{1,2,0:T(8,128)(2,1)}, u32[]{:S(2)}, u32[]{:S(2)}) async-start(bf16[4,128,384]{1,2,0:T(8,128)(2,1)} %copy.32), calls=%async_computation | async-start | bytes 786432 | tf_op jit(solution)/shard_map/all_to_all | solution.py:196
  69.7 0.0 all-gather.12.cloned.1.call-start
  69.7 6.7 %all-to-all-done = bf16[4,128,384]{1,2,0:T(8,128)(2,1)} async-done(((bf16[4,128,384]{1,2,0:T(8,128)(2,1)}), bf16[4,128,384]{1,2,0:T(8,128)(2,1)}, u32[]{:S(2)}, u32[]{:S(2)}) %all-to-all-start) | async-done | bytes 393248 | tf_op jit(solution)/shard_map/all_to_all | solution.py:196
  76.3 3.4 %multiply_reduce_fusion = (f32[128]{0:T(128)S(1)}, f32[128,1536]{1,0:T(8,128)S(1)}) fusion(bf16[128,1536]{0,1:T(8,128)(2,1)} %bitcast.4, bf16[1536,1536]{1,0:T(8,128)(2,1)} %all-gather.10.cloned.1.call-done, bf16[512,1536]{1,0:T(8,128)(2,1)S(1)} %copy-done.3, s32[]{:T(128)S(6)} %select_n.25), kind=kOutput, calls=%fused_computation.37 | convolution fusion | flops 605159296 | bytes 6291972 | tf_op jit(solution)/shard_map/dot_general | solution.py:200
  79.7 0.0 copy-done.4
  79.7 0.9 multiply_convert_fusion
  80.6 0.0 all-gather.12.cloned.1.call-update
  80.6 0.0 all-gather.16.cloned.1.call-start
  80.7 0.5 all-gather.16.cloned.1.call-update
  81.2 0.0 all-gather.18.cloned.1.call-start
  81.3 0.5 all-gather.18.cloned.1.call-update
  81.8 0.0 reduce-scatter.2.cloned.1.call-start
  81.9 0.7 constant_dynamic-slice_fusion.1
  82.6 0.7 constant_dynamic-slice_fusion.2
  83.3 24.2 %all_gather.23 = f32[1024,8]{0,1:T(8,128)S(1)} all-gather(f32[128,8]{0,1:T(8,128)S(1)} %select_reduce_fusion), channel_id=1, replica_groups=mesh['expert'=8,'tensor'=4] {'expert'}, dimensions={0}, use_global_device_ids=true | all-gather | bytes 36864 | tf_op jit(solution)/shard_map/all_gather | solution.py:172
  107.5 0.0 all-gather.14.cloned.1.call-done
  107.5 53.8 %all-gather.12.cloned.1.call-done = bf16[1024,1536]{1,0:T(8,128)(2,1)} async-done(((bf16[128,1536]{1,0:T(8,128)(2,1)}), bf16[1024,1536]{1,0:T(8,128)(2,1)}) %all-gather.12.cloned.1.call-update) | async-done | bytes 3145744 | tf_op jit(solution)/shard_map/all_gather | solution.py:203
  161.3 4.2 %convolution_maximum_fusion.3 = f32[1024,192]{0,1:T(8,128)} fusion(bf16[1024,1536]{1,0:T(8,128)(2,1)} %all-gather.12.cloned.1.call-done, bf16[4,1536,192]{1,2,0:T(8,128)(2,1)} %all-gather.14.cloned.1.call-done), kind=kOutput, calls=%fused_computation.24 | convolution fusion | flops 604176384 | bytes 4521984 | tf_op jit(solution)/shard_map/dot_general | solution.py:207
  165.5 0.0 copy-done.5
  165.5 0.0 copy-done.7
  165.5 2.1 convolution_maximum_fusion.2
  167.6 1.2 convolution_maximum_fusion.1
  168.8 1.2 convolution_maximum_fusion
  170.0 16.7 %all-gather.16.cloned.1.call-done = bf16[4,1536,192]{1,2,0:T(8,128)(2,1)} async-done(((bf16[1,1536,192]{1,2,0:T(8,128)(2,1)}), bf16[4,1536,192]{1,2,0:T(8,128)(2,1)}) %all-gather.16.cloned.1.call-update) | async-done | bytes 2359312 | tf_op jit(solution)/shard_map/all_gather | solution.py:165
  186.7 4.3 %fusion.13 = bf16[1024,192]{0,1:T(8,128)(2,1)} fusion(f32[1024,192]{0,1:T(8,128)} %convolution_maximum_fusion.3, bf16[1024,1536]{1,0:T(8,128)(2,1)} %all-gather.12.cloned.1.call-done, bf16[4,1536,192]{1,2,0:T(8,128)(2,1)} %all-gather.16.cloned.1.call-done), kind=kOutput, calls=%fused_computation.25 | convolution fusion | flops 604372992 | bytes 4915200 | tf_op jit(solution)/shard_map/dot_general | solution.py:208
  191.0 0.0 copy-done.6
  191.0 0.0 copy-done.8
  191.0 0.0 copy-done.10
  191.0 1.9 fusion.14
  193.0 1.9 fusion.15
  194.9 1.9 fusion.16
  196.8 15.4 %all-gather.18.cloned.1.call-done = bf16[1,768,1536]{2,1,0:T(8,128)(2,1)} async-done(((bf16[1,192,1536]{2,1,0:T(8,128)(2,1)}), bf16[1,768,1536]{2,1,0:T(8,128)(2,1)}) %all-gather.18.cloned.1.call-update) | async-done | bytes 2359312 | tf_op jit(solution)/shard_map/all_gather | solution.py:166
  212.2 0.0 copy-done.11
  212.2 0.0 copy-done.12
  212.2 6.3 %select_convert_fusion = bf16[1024,1536]{1,0:T(8,128)(2,1)} fusion(f32[1024]{0:T(1024)S(1)} %bitcast.57, pred[1024]{0:T(1024)(128)(4,1)S(1)} %get-tuple-element.5, bf16[1,768,1536]{2,1,0:T(8,128)(2,1)} %all-gather.18.cloned.1.call-done, bf16[1024,192]{0,1:T(8,128)(2,1)} %fusion.16, bf16[1024,192]{0,1:T(8,128)(2,1)} %fusion.15, ...), kind=kOutput, calls=%fused_computation | convolution fusion | flops 2426929152 | bytes 7083008 | tf_op jit(solution)/shard_map/dot_general | solution.py:211
  218.5 0.0 reduce-scatter.2.cloned.1.call-update
  218.5 73.3 %reduce-scatter.2.cloned.1.call-done = bf16[128,1536]{1,0:T(8,128)(2,1)} async-done(((bf16[1024,1536]{1,0:T(8,128)(2,1)}), bf16[128,1536]{1,0:T(8,128)(2,1)}) %reduce-scatter.2.cloned.1.call-update) | async-done | bytes 393232 | tf_op jit(solution)/shard_map/reduce_scatter | solution.py:213
  291.8 1.1 add_convert_fusion
  292.9 10.3 %all_to_all.38 = bf16[128,4,384]{2,0,1:T(8,128)(2,1)S(1)} all-to-all(bf16[128,4,384]{2,0,1:T(8,128)(2,1)S(1)} %bitcast.54), channel_id=1, replica_groups=mesh['expert'=8,'tensor'=4] {'tensor'}, dimensions={1} | all-to-all | bytes 786432 | tf_op jit(solution)/shard_map/all_to_all | solution.py:215
  303.3 0.7 copy.41
  (15 shorter events, 0.1 us)
Async XLA Ops:
  6.5 28.7 %copy-start = (bf16[1536,384]{1,0:T(8,128)(2,1)S(1)}, bf16[1536,384]{1,0:T(8,128)(2,1)}, u32[]{:S(2)}) copy-start(bf16[1536,384]{1,0:T(8,128)(2,1)} %param.22) | copy-start | bytes 3538948
  6.5 26.3 %copy-start.9 = (f32[1536]{0:T(1024)S(1)}, f32[1536]{0:T(1024)}, u32[]{:S(2)}) copy-start(f32[1536]{0:T(1024)} %param.21) | copy-start | bytes 18436
  6.5 24.5 %all-gather.8.cloned.1.call-start = ((), (), s32[]{:S(2)}) async-start(), calls=%async_computation.3 | async-start | bytes 1966080 | tf_op jit(solution)/shard_map/all_gather | solution.py:162
  7.3 69.1 %all-gather.10.cloned.1.call-start = ((), (), s32[]{:S(2)}) async-start(), calls=%async_computation.4 | async-start | bytes 5898240 | tf_op jit(solution)/shard_map/all_gather | solution.py:163
  8.0 99.5 %all-gather.14.cloned.1.call-start = ((), (), s32[]{:S(2)}) async-start(), calls=%async_computation.6 | async-start | bytes 2949120 | tf_op jit(solution)/shard_map/all_gather | solution.py:164
  32.9 2.4 copy-start.3
  32.9 3.3 %copy-start.2 = (bf16[1,8192,256]{2,1,0:T(8,128)(2,1)S(1)}, bf16[1,8192,256]{2,1,0:T(8,128)(2,1)}, u32[]{:S(2)}) copy-start(bf16[1,8192,256]{2,1,0:T(8,128)(2,1)} %v_ref.1) | copy-start | bytes 12582916
  35.2 2.4 copy-start.1
  65.3 11.0 %all-to-all-start = ((bf16[4,128,384]{1,2,0:T(8,128)(2,1)}), bf16[4,128,384]{1,2,0:T(8,128)(2,1)}, u32[]{:S(2)}, u32[]{:S(2)}) async-start(bf16[4,128,384]{1,2,0:T(8,128)(2,1)} %copy.32), calls=%async_computation | async-start | bytes 786432 | tf_op jit(solution)/shard_map/all_to_all | solution.py:196
  69.7 91.7 %all-gather.12.cloned.1.call-start = ((), (), s32[]{:S(2)}) async-start(), calls=%async_computation.5 | async-start | bytes 3538944 | tf_op jit(solution)/shard_map/all_gather | solution.py:203
  76.3 3.4 %copy-start.4 = (f32[1536]{0:T(1024)S(1)}, f32[1536]{0:T(1024)}, u32[]{:S(2)}) copy-start(f32[1536]{0:T(1024)} %param.26) | copy-start | bytes 18436
  80.6 106.0 %all-gather.16.cloned.1.call-start = ((), (), s32[]{:S(2)}) async-start(), calls=%async_computation.7 | async-start | bytes 2949120 | tf_op jit(solution)/shard_map/all_gather | solution.py:165
  81.2 131.0 %all-gather.18.cloned.1.call-start = ((), (), s32[]{:S(2)}) async-start(), calls=%async_computation.9 | async-start | bytes 2949120 | tf_op jit(solution)/shard_map/all_gather | solution.py:166
  81.8 210.0 %reduce-scatter.2.cloned.1.call-start = ((), (), s32[]{:S(2)}) async-start(), calls=%async_computation.8 | async-start | bytes 3538944 | tf_op jit(solution)/shard_map/reduce_scatter | solution.py:213
  161.3 4.2 %copy-start.5 = (bf16[1024,1536]{1,0:T(8,128)(2,1)S(1)}, bf16[1024,1536]{1,0:T(8,128)(2,1)}, u32[]{:S(2)}) copy-start(bf16[1024,1536]{1,0:T(8,128)(2,1)} %all-gather.12.cloned.1.call-done) | copy-start | bytes 9437188
  161.3 4.2 %copy-start.7 = (bf16[4,1536,192]{1,2,0:T(8,128)(2,1)S(1)}, bf16[4,1536,192]{1,2,0:T(8,128)(2,1)}, u32[]{:S(2)}) copy-start(bf16[4,1536,192]{1,2,0:T(8,128)(2,1)} %all-gather.14.cloned.1.call-done) | copy-start | bytes 7077892
  186.7 4.3 %copy-start.6 = (bf16[1024,1536]{1,0:T(8,128)(2,1)S(1)}, bf16[1024,1536]{1,0:T(8,128)(2,1)}, u32[]{:S(2)}) copy-start(bf16[1024,1536]{1,0:T(8,128)(2,1)} %all-gather.12.cloned.1.call-done) | copy-start | bytes 9437188
  186.7 4.3 %copy-start.8 = (bf16[4,1536,192]{1,2,0:T(8,128)(2,1)S(1)}, bf16[4,1536,192]{1,2,0:T(8,128)(2,1)}, u32[]{:S(2)}) copy-start(bf16[4,1536,192]{1,2,0:T(8,128)(2,1)} %all-gather.16.cloned.1.call-done) | copy-start | bytes 7077892
  186.7 4.3 %copy-start.10 = (f32[1024,192]{0,1:T(8,128)S(1)}, f32[1024,192]{0,1:T(8,128)}, u32[]{:S(2)}) copy-start(f32[1024,192]{0,1:T(8,128)} %convolution_maximum_fusion.2) | copy-start | bytes 2359300
  194.9 17.3 %copy-start.11 = (bf16[1024,192]{0,1:T(8,128)(2,1)S(1)}, bf16[1024,192]{0,1:T(8,128)(2,1)}, u32[]{:S(2)}) copy-start(bf16[1024,192]{0,1:T(8,128)(2,1)} %fusion.13) | copy-start | bytes 1179652
  194.9 17.3 %copy-start.12 = (bf16[1024,192]{0,1:T(8,128)(2,1)S(1)}, bf16[1024,192]{0,1:T(8,128)(2,1)}, u32[]{:S(2)}) copy-start(bf16[1024,192]{0,1:T(8,128)(2,1)} %fusion.14) | copy-start | bytes 1179652
Sparse Core Ops, SparseCore 0:
  8.9 22.1 all-gather.7
  32.6 37.4 all-gather.9
  71.7 28.2 all-gather.13
  102.1 59.2 all-gather.11
  162.7 23.9 all-gather.15
  188.1 24.0 all-gather.17
  218.6 73.1 reduce-scatter.1

commit v2 on v1

--- a/solution.py
+++ b/solution.py
@@ -131,6 +131,258 @@
     )(info, queries_t, new_keys, new_values, keys, values)
 
 
+def tail_kernel(
+    groups,
+    context,
+    base,
+    table,
+    gain,
+    w_out,
+    gate,
+    up,
+    down,
+    out_ref,
+    ctx_in,
+    rows_g,
+    rows_p,
+    tab_g,
+    tab_p,
+    keep,
+    out_y,
+    in_y,
+    in_z,
+    residual,
+    pieces,
+    ctx_send,
+    ctx_recv,
+    row_send,
+    row_recv,
+    tab_send,
+    tab_recv,
+    y_send,
+    y_recv,
+    z_send,
+    z_recv,
+    end_send,
+    end_recv,
+):
+    tensor_count = lax.axis_size("tensor")
+    tensor = lax.axis_index("tensor")
+    expert = lax.axis_index("expert")
+    group = expert // 2
+    side = expert % 2
+    partner = (group * 2 + (1 - side), tensor)
+    quarter = base.shape[0]
+    width = out_ref.shape[1]
+
+    def peer(step):
+        return (expert, (tensor + step) % tensor_count)
+
+    def ahead(step):
+        return (((group + step) % groups) * 2 + side, tensor)
+
+    def behind(step):
+        return (((group + groups - step) % groups) * 2 + side, tensor)
+
+    def remote(source, target, send, recv, device):
+        return pltpu.make_async_remote_copy(
+            src_ref=source,
+            dst_ref=target,
+            send_sem=send,
+            recv_sem=recv,
+            device_id=device,
+            device_id_type=pl.DeviceIdType.MESH,
+        )
+
+    def context_copy(step):
+        place = ((tensor + step) % tensor_count) * quarter
+        return remote(
+            context.at[pl.ds(pl.multiple_of(place, quarter), quarter)],
+            ctx_in.at[step],
+            ctx_send.at[step],
+            ctx_recv.at[step],
+            peer(step),
+        )
+
+    def group_copies(step):
+        return (
+            remote(rows_g.at[0], rows_g.at[step], row_send.at[0, step], row_recv.at[0, step], ahead(step)),
+            remote(tab_g.at[0], tab_g.at[step], tab_send.at[0, step], tab_recv.at[0, step], ahead(step)),
+        )
+
+    def partner_copies(step):
+        return (
+            remote(rows_g.at[step], rows_p.at[step], row_send.at[1, step], row_recv.at[1, step], partner),
+            remote(tab_g.at[step], tab_p.at[step], tab_send.at[1, step], tab_recv.at[1, step], partner),
+        )
+
+    def y_copy(step):
+        return remote(out_y.at[step], in_y.at[step], y_send.at[step], y_recv.at[step], partner)
+
+    def z_copy(step):
+        return remote(in_y.at[step], in_z.at[step], z_send.at[step], z_recv.at[step], behind(step))
+
+    def end_copy(step):
+        place = (tensor + step) % tensor_count
+        return remote(
+            pieces.at[place],
+            out_ref.at[pl.ds(pl.multiple_of(tensor * quarter, quarter), quarter)],
+            end_send.at[step],
+            end_recv.at[step],
+            peer(step),
+        )
+
+    barrier = pltpu.get_barrier_semaphore()
+
+    def greet(device):
+        pl.semaphore_signal(
+            barrier, inc=1, device_id=device, device_id_type=pl.DeviceIdType.MESH
+        )
+
+    greet(partner)
+    for step in range(1, groups):
+        greet(ahead(step))
+    for step in range(1, tensor_count):
+        greet(peer(step))
+    pl.semaphore_wait(barrier, groups + tensor_count - 1)
+
+    for step in range(1, tensor_count):
+        context_copy(step).start()
+    mine = context[pl.ds(pl.multiple_of(tensor * quarter, quarter), quarter), :]
+    total = base[...].astype(jnp.float32) + jnp.dot(
+        mine, w_out[tensor], preferred_element_type=jnp.float32
+    )
+    for step in range(1, tensor_count):
+        context_copy(step).wait_recv()
+        source = (tensor + tensor_count - step) % tensor_count
+        total = total + jnp.dot(ctx_in[step], w_out[source], preferred_element_type=jnp.float32)
+    residual[...] = total.astype(jnp.bfloat16)
+    values = residual[...].astype(jnp.float32)
+    mean_square = jnp.mean(values * values, axis=-1, keepdims=True)
+    rows_g[0] = (values * lax.rsqrt(mean_square + epsilon) * gain[...]).astype(jnp.bfloat16)
+    tab_g[0] = table[...]
+
+    for step in range(1, groups):
+        for copy in group_copies(step):
+            copy.start()
+    for copy in partner_copies(0):
+        copy.start()
+
+    def column(tab):
+        place = lax.broadcasted_iota(jnp.int32, tab.shape, 0)
+        row = jnp.sum(jnp.where(place == expert, tab, 0.0), axis=0, keepdims=True)
+        return jnp.broadcast_to(row, (8, quarter)).T[:, :1]
+
+    def merge(step):
+        y_copy(step).wait_recv()
+        joined = keep[step % 2] + in_y[step].astype(jnp.float32)
+        in_y[step] = joined.astype(jnp.bfloat16)
+
+        @pl.when(step > 0)
+        def _():
+            z_copy(step).start()
+
+    def visit(step, carry):
+        @pl.when(step + 1 < groups)
+        def _():
+            for copy in group_copies(step + 1):
+                copy.wait_recv()
+            for copy in partner_copies(step + 1):
+                copy.start()
+
+        for copy in partner_copies(step):
+            copy.wait_recv()
+        rows = jnp.concatenate([rows_g[step], rows_p[step]], axis=0)
+        result = None
+        for part in range(tensor_count):
+            gated = jnp.dot(rows, gate[part], preferred_element_type=jnp.float32)
+            upward = jnp.dot(rows, up[part], preferred_element_type=jnp.float32)
+            active = (jnp.maximum(gated, 0.0) * upward).astype(jnp.bfloat16)
+            term = jnp.dot(active, down[part], preferred_element_type=jnp.float32)
+            result = term if result is None else result + term
+        out_y[step] = (result[quarter:] * column(tab_p[step])).astype(jnp.bfloat16)
+        y_copy(step).start()
+        keep[step % 2] = result[:quarter] * column(tab_g[step])
+
+        @pl.when(step > 0)
+        def _():
+            merge(step - 1)
+
+        return carry
+
+    lax.fori_loop(0, groups, visit, 0)
+    merge(groups - 1)
+
+    final = residual[...].astype(jnp.float32) + in_y[0].astype(jnp.float32)
+    for step in range(1, groups):
+        z_copy(step).wait_recv()
+        final = final + in_z[step].astype(jnp.float32)
+    final = final.astype(jnp.bfloat16)
+    for part in range(tensor_count):
+        pieces[part] = final[:, part * width : (part + 1) * width]
+    for step in range(1, tensor_count):
+        end_copy(step).start()
+    out_ref[pl.ds(pl.multiple_of(tensor * quarter, quarter), quarter), :] = pieces[tensor]
+
+    for step in range(1, tensor_count):
+        end_copy(step).wait_recv()
+        end_copy(step).wait_send()
+        context_copy(step).wait_send()
+    for step in range(groups):
+        for copy in partner_copies(step):
+            copy.wait_send()
+        y_copy(step).wait_send()
+        if step > 0:
+            for copy in group_copies(step):
+                copy.wait_send()
+            z_copy(step).wait_send()
+
+
+def tail(context, base, table, gain, w_out, gate, up, down):
+    groups = lax.axis_size("expert") // 2
+    tensor_count = lax.axis_size("tensor")
+    quarter, model = base.shape
+    width = model // tensor_count
+    dma = pltpu.SemaphoreType.DMA
+    block = (groups, quarter, model)
+    operands = (context, base, table, gain, w_out, gate, up, down)
+    return pl.pallas_call(
+        functools.partial(tail_kernel, groups),
+        out_shape=jax.ShapeDtypeStruct((quarter * tensor_count, width), jnp.bfloat16),
+        in_specs=[pl.BlockSpec(memory_space=pltpu.VMEM)] * len(operands),
+        out_specs=pl.BlockSpec(memory_space=pltpu.VMEM),
+        scratch_shapes=[
+            pltpu.VMEM((tensor_count, quarter, context.shape[1]), jnp.bfloat16),
+            pltpu.VMEM(block, jnp.bfloat16),
+            pltpu.VMEM(block, jnp.bfloat16),
+            pltpu.VMEM((groups,) + table.shape, jnp.float32),
+            pltpu.VMEM((groups,) + table.shape, jnp.float32),
+            pltpu.VMEM((2, quarter, model), jnp.float32),
+            pltpu.VMEM(block, jnp.bfloat16),
+            pltpu.VMEM(block, jnp.bfloat16),
+            pltpu.VMEM(block, jnp.bfloat16),
+            pltpu.VMEM((quarter, model), jnp.bfloat16),
+            pltpu.VMEM((tensor_count, quarter, width), jnp.bfloat16),
+            dma((tensor_count,)),
+            dma((tensor_count,)),
+            dma((2, groups)),
+            dma((2, groups)),
+            dma((2, groups)),
+            dma((2, groups)),
+            dma((groups,)),
+            dma((groups,)),
+            dma((groups,)),
+            dma((groups,)),
+            dma((tensor_count,)),
+            dma((tensor_count,)),
+        ],
+        compiler_params=pltpu.CompilerParams(
+            collective_id=0, has_side_effects=True, vmem_limit_bytes=56 * 1024 * 1024
+        ),
+        name="tail",
+    )(*operands)
+
+
 def local(
     hidden_in,
     cache_lengths,
@@ -151,7 +403,6 @@
 ):
     tensor_count = lax.axis_size("tensor")
     tensor_index = lax.axis_index("tensor")
-    expert_index = lax.axis_index("expert")
     new_count = hidden_in.shape[0]
     quarter = new_count // tensor_count
     local_heads = w_query.shape[1] // HEAD_DIM
@@ -160,17 +411,15 @@
     expert_total = w_gate.shape[0] * lax.axis_size("expert")
 
     full_rows = lax.all_gather(hidden_in, "tensor", axis=1, tiled=True)
-    whole_out = lax.all_gather(w_out, "tensor", axis=0, tiled=True)
+    whole_out = lax.all_gather(w_out, "tensor", axis=0, tiled=False)
     whole_gate = lax.all_gather(w_gate[0], "tensor", axis=0, tiled=False)
     whole_up = lax.all_gather(w_up[0], "tensor", axis=0, tiled=False)
-    whole_down = lax.all_gather(w_down[0], "tensor", axis=0, tiled=True)
+    whole_down = lax.all_gather(w_down[0], "tensor", axis=0, tiled=False)
 
     my_ids = lax.dynamic_slice_in_dim(route_ids, tensor_index * quarter, quarter, 0)
     my_weights = lax.dynamic_slice_in_dim(route_weights, tensor_index * quarter, quarter, 0)
-    named = my_ids[:, :, None] == jnp.arange(expert_total, dtype=jnp.int32)[None, None, :]
-    table = jnp.sum(jnp.where(named, my_weights[:, :, None], 0.0), axis=1)
-    tables = lax.all_gather(table, "expert", axis=0, tiled=True)
-    row_weight = lax.dynamic_slice_in_dim(tables, expert_index, 1, 1)
+    named = my_ids.T[:, None, :] == jnp.arange(expert_total, dtype=jnp.int32)[None, :, None]
+    table = jnp.sum(jnp.where(named, my_weights.T[:, None, :], 0.0), axis=0)
 
     attn_in = norm_rows(full_rows, attn_gain)
     queries_t = lax.dot_general(
@@ -193,26 +442,17 @@
         new_lengths[0],
         shared,
     )
-    my_context = lax.all_to_all(context, "tensor", split_axis=0, concat_axis=1, tiled=True)
     my_rows = lax.dynamic_slice_in_dim(full_rows, tensor_index * quarter, quarter, 0)
-    residual = (
-        my_rows.astype(jnp.float32)
-        + jnp.dot(my_context, whole_out, preferred_element_type=jnp.float32)
-    ).astype(jnp.bfloat16)
-    moe_rows = norm_rows(residual, moe_gain)
-    all_rows = lax.all_gather(moe_rows, "expert", axis=0, tiled=True)
-    partial = jnp.zeros((all_rows.shape[0], all_rows.shape[1]), jnp.float32)
-    actives = []
-    for part in range(tensor_count):
-        gate_value = jnp.dot(all_rows, whole_gate[part], preferred_element_type=jnp.float32)
-        upward = jnp.dot(all_rows, whole_up[part], preferred_element_type=jnp.float32)
-        actives.append((jnp.maximum(gate_value, 0.0) * upward).astype(jnp.bfloat16))
-    active = jnp.concatenate(actives, axis=1)
-    partial = jnp.dot(active, whole_down, preferred_element_type=jnp.float32)
-    weighted = jnp.where(row_weight > 0.0, partial * row_weight, 0.0).astype(jnp.bfloat16)
-    summed = lax.psum_scatter(weighted, "expert", scatter_dimension=0, tiled=True)
-    mixed = (residual.astype(jnp.float32) + summed.astype(jnp.float32)).astype(jnp.bfloat16)
-    return lax.all_to_all(mixed, "tensor", split_axis=1, concat_axis=0, tiled=True)
+    return tail(
+        context,
+        my_rows,
+        table,
+        moe_gain[None, :],
+        whole_out,
+        whole_gate,
+        whole_up,
+        whole_down,
+    )
 
 
 def solution(mesh):

time: 312 us -> 267 us (0.86)
  Pallas kernels: 26.8 us -> 136 us
  waiting for transfers between devices: 188 us -> 95.1 us
  blocking collectives: 34.5 us -> 0 us
  matrix products: 31.5 us -> 3.14 us
  local copies, waits for them, and re-layouts: 6.51 us -> 15.7 us
  starting transfers between devices: 4.54 us -> 0.18 us
    pallas_call x0 -> x1, Pallas kernels: none -> 112 us  [tail(): pl.pallas_call(functools.partial(tail_kernel, groups), out_shape=jax.Shap...]
    reduce_scatter x1 -> x0, waiting for transfers between devices: 73.3 us -> none  [local(): lax.psum_scatter(weighted, 'expert', scatter_dimension=0, tiled=True)]
    dot_general x10 -> x0, matrix products: 28.4 us -> none  [the longest x4 10.1 us: local(): jnp.dot(all_rows, whole_up[part], preferred_element_type=jnp.float32)]
    all_gather x1 -> x0, blocking collectives: 24.2 us -> none  [local(): tables = lax.all_gather(table, 'expert', axis=0, tiled=True)]
    all_to_all x1 -> x0, blocking collectives: 10.3 us -> none  [local(): lax.all_to_all(mixed, 'tensor', split_axis=1, concat_axis=0, tiled=True)]
    all_gather x3 -> x2, waiting for transfers between devices: 69.2 us -> 59.9 us  [the longest x1 38.9 us: local(): whole_out = lax.all_gather(w_out, 'tensor', axis=0, tiled=False)]
    all_gather x0 -> x2, local copies, waits for them, and re-layouts: none -> 9.09 us  [the longest x1 4.56 us: local(): whole_up = lax.all_gather(w_up[0], 'tensor', axis=0, tiled=False)]
    all_to_all x1 -> x0, waiting for transfers between devices: 6.68 us -> none  [local(): lax.all_to_all(context, 'tensor', split_axis=0, concat_axis=1, tiled=True)]
  transfers between devices with their start and end apart: 8 -> 5, of which waited for: 6 -> 4; matrix products, arithmetic and copies ran while one was open for 10% -> 7% of each run, Pallas kernels for 9% -> 9%
where the time goes in v2:
time: 267 us
  Pallas kernels  136 us (51%)
  waiting for transfers between devices  95.1 us (36%)
  local copies, waits for them, and re-layouts  15.7 us (6%)
  between operations  14.6 us (5%)
  matrix products  3.14 us (1%)
    pallas_call x1, Pallas kernels, tail(): pl.pallas_call(functools.partial(tail_kernel, groups), out_shape=jax.Shap...  112 us
    all_gather x1, waiting for transfers between devices, local(): whole_out = lax.all_gather(w_out, 'tensor', axis=0, tiled=False)  38.9 us
    pallas_call x1, Pallas kernels, attention(): pl.pallas_call(functools.partial(attention_kernel, heads, scale), grid_sp...  23.9 us
    all_gather x1, waiting for transfers between devices, local(): whole_down = lax.all_gather(w_down[0], 'tensor', axis=0, tiled=False)  21 us
    all_gather x1, waiting for transfers between devices, local(): full_rows = lax.all_gather(hidden_in, 'tensor', axis=1, tiled=True)  17.1 us
    all_gather x1, waiting for transfers between devices, local(): whole_up = lax.all_gather(w_up[0], 'tensor', axis=0, tiled=False)  14.9 us
  transfers between devices with their start and end apart: 5, of which 4 were waited for; matrix products, arithmetic and copies ran while one was open for 7% of the time, Pallas kernels for 9%

profile of v2, /device:TPU:1, one launch (start us, length us, event | category | flops | bytes accessed | tf_op | source)
XLA Modules:
  0.0 267.1 jit_solution(9179367900587432336)
XLA Ops:
  6.5 0.0 copy-start
  6.5 0.0 copy-start.7
  6.5 0.0 copy-start.6
  6.5 0.0 copy-start.5
  6.5 0.0 all-gather.7.cloned.1.call-start
  6.6 0.7 all-gather.7.cloned.1.call-update
  7.3 0.0 all-gather.9.cloned.1.call-start
  7.3 0.7 all-gather.9.cloned.1.call-update
  8.0 0.0 all-gather.11.cloned.1.call-start
  8.1 0.7 all-gather.11.cloned.1.call-update
  8.8 0.0 copy-start.8
  8.8 0.0 all-gather.13.cloned.1.call-start
  8.8 0.5 all-gather.13.cloned.1.call-update
  9.3 0.0 all-gather.15.cloned.1.call-start
  9.4 0.5 all-gather.15.cloned.1.call-update
  11.3 0.0 copy-done.7
  11.3 0.6 broadcast_in_dim.22.gain
  11.9 0.1 pad_add_fusion.info
  11.9 0.7 dynamic-slice_bitcast_fusion
  12.6 0.7 dynamic-slice_bitcast_fusion.1
  13.3 0.6 select_reduce_fusion.table
  13.9 0.0 copy-done.6
  13.9 0.0 copy-done.5
  13.9 0.1 constant_dynamic-slice_fusion.1
  14.0 17.1 %all-gather.7.cloned.1.call-done = bf16[512,1536]{1,0:T(8,128)(2,1)} async-done(((bf16[512,384]{1,0:T(8,128)(2,1)}), bf16[512,1536]{1,0:T(8,128)(2,1)}) %all-gather.7.cloned.1.call-update) | async-done | bytes 1572880 | tf_op jit(solution)/shard_map/all_gather | solution.py:413
  31.1 0.0 copy-start.4
  31.1 1.9 fusion
  33.0 0.0 copy-done.8
  33.0 0.0 copy-start.3
  33.0 2.2 convolution_convert_fusion.1
  35.3 0.0 copy-done.4
  35.3 0.8 constant_dynamic-slice_fusion.base
  36.1 0.0 copy-done
  36.1 0.0 copy-start.2
  36.1 0.9 fusion.3.q_ref
  37.0 0.0 copy-done.3
  37.0 1.2 copy-done.2
  38.3 23.9 %attention.1.context = bf16[512,384]{1,0:T(8,128)(2,1)S(1)} custom-call(s32[3]{0:T(128)S(1)} %pad_add_fusion.info, bf16[384,512]{1,0:T(8,128)(2,1)S(1)} %fusion.3.q_ref, bf16[512,128]{1,0:T(8,128)(2,1)S(1)} %get-tuple-element.6.nk_ref, bf16[512,128]{1,0:T(8,128)(2,1)S(1)} %get-tuple-element.5.nv_ref, bf16[1,8192,256]{2,1,0:T(8,128)(2,1)S(1)} %copy-done.2, ...), custom_call_target="tpu_custom_call" | custom-call | flops 6442450944 | bytes 4194304 | tf_op jit(solution)/shard_map/attention/pallas_call | solution.py:104
  62.2 0.0 copy-start.1
  62.2 0.7 copy-done.1
  62.9 0.0 all-gather.9.cloned.1.call-done
  63.0 4.5 %copy.24.gate = bf16[4,1536,192]{2,1,0:T(8,128)(2,1)} copy(bf16[4,1536,192]{1,2,0:T(8,128)(2,1)} %all-gather.9.cloned.1.call-done) | data formatting | bytes 4718592 | tf_op jit(solution)/shard_map/all_gather | solution.py:415
  67.5 14.9 %all-gather.11.cloned.1.call-done = bf16[4,1536,192]{1,2,0:T(8,128)(2,1)} async-done(((bf16[1,1536,192]{1,2,0:T(8,128)(2,1)}), bf16[4,1536,192]{1,2,0:T(8,128)(2,1)}) %all-gather.11.cloned.1.call-update) | async-done | bytes 2359312 | tf_op jit(solution)/shard_map/all_gather | solution.py:416
  82.4 4.6 %copy.25.up = bf16[4,1536,192]{2,1,0:T(8,128)(2,1)} copy(bf16[4,1536,192]{1,2,0:T(8,128)(2,1)} %all-gather.11.cloned.1.call-done) | data formatting | bytes 4718592 | tf_op jit(solution)/shard_map/all_gather | solution.py:416
  87.0 21.0 %all-gather.13.cloned.1.call-done.down = bf16[4,192,1536]{2,1,0:T(8,128)(2,1)} async-done(((bf16[1,192,1536]{2,1,0:T(8,128)(2,1)}), bf16[4,192,1536]{2,1,0:T(8,128)(2,1)}) %all-gather.13.cloned.1.call-update) | async-done | bytes 2359312 | tf_op jit(solution)/shard_map/all_gather | solution.py:417
  107.9 38.9 %all-gather.15.cloned.1.call-done = bf16[1536,1536]{1,0:T(8,128)(2,1)} async-done(((bf16[384,1536]{1,0:T(8,128)(2,1)}), bf16[1536,1536]{1,0:T(8,128)(2,1)}) %all-gather.15.cloned.1.call-update) | async-done | bytes 4718608 | tf_op jit(solution)/shard_map/all_gather | solution.py:414
  146.9 111.9 %tail.1 = bf16[512,384]{1,0:T(8,128)(2,1)} custom-call(bf16[512,384]{1,0:T(8,128)(2,1)} %copy-done.1, bf16[128,1536]{1,0:T(8,128)(2,1)} %constant_dynamic-slice_fusion.base, f32[8,128]{1,0:T(8,128)} %select_reduce_fusion.table, f32[1,1536]{1,0:T(1,128)} %broadcast_in_dim.22.gain, bf16[4,384,1536]{2,1,0:T(8,128)(2,1)} %bitcast.9, ...), custom_call_target="tpu_custom_call" | custom-call | tf_op jit(solution)/shard_map/tail/pallas_call | solution.py:349
  258.8 1.8 copy.30
  (2 shorter events, 0.0 us)
Async XLA Ops:
  6.5 29.5 %copy-start = (bf16[1536,384]{1,0:T(8,128)(2,1)S(1)}, bf16[1536,384]{1,0:T(8,128)(2,1)}, u32[]{:S(2)}) copy-start(bf16[1536,384]{1,0:T(8,128)(2,1)} %param.22) | copy-start | bytes 3538948
  6.5 4.7 %copy-start.7 = (f32[1536]{0:T(1024)S(1)}, f32[1536]{0:T(1024)}, u32[]{:S(2)}) copy-start(f32[1536]{0:T(1024)} %param.26) | copy-start | bytes 18436
  6.5 7.4 %copy-start.6 = (bf16[1536,256]{1,0:T(8,128)(2,1)S(1)}, bf16[1536,256]{1,0:T(8,128)(2,1)}, u32[]{:S(2)}) copy-start(bf16[1536,256]{1,0:T(8,128)(2,1)} %param.23) | copy-start | bytes 2359300
  6.5 7.4 %copy-start.5 = (bf16[1536,256]{1,0:T(8,128)(2,1)S(1)}, bf16[1536,256]{1,0:T(8,128)(2,1)}, u32[]{:S(2)}) copy-start(bf16[1536,256]{1,0:T(8,128)(2,1)} %param.24) | copy-start | bytes 2359300
  6.5 24.5 %all-gather.7.cloned.1.call-start = ((), (), s32[]{:S(2)}) async-start(), calls=%async_computation | async-start | bytes 1966080 | tf_op jit(solution)/shard_map/all_gather | solution.py:413
  7.3 55.7 %all-gather.9.cloned.1.call-start = ((), (), s32[]{:S(2)}) async-start(), calls=%async_computation.1 | async-start | bytes 2949120 | tf_op jit(solution)/shard_map/all_gather | solution.py:415
  8.0 74.4 %all-gather.11.cloned.1.call-start = ((), (), s32[]{:S(2)}) async-start(), calls=%async_computation.2 | async-start | bytes 2949120 | tf_op jit(solution)/shard_map/all_gather | solution.py:416
  8.8 24.2 %copy-start.8 = (f32[1536]{0:T(1024)S(1)}, f32[1536]{0:T(1024)}, u32[]{:S(2)}) copy-start(f32[1536]{0:T(1024)} %param.21) | copy-start | bytes 18436
  8.8 99.2 %all-gather.13.cloned.1.call-start = ((), (), s32[]{:S(2)}) async-start(), calls=%async_computation.3 | async-start | bytes 2949120 | tf_op jit(solution)/shard_map/all_gather | solution.py:417
  9.3 137.5 %all-gather.15.cloned.1.call-start = ((), (), s32[]{:S(2)}) async-start(), calls=%async_computation.4 | async-start | bytes 5898240 | tf_op jit(solution)/shard_map/all_gather | solution.py:414
  31.1 4.2 %copy-start.4 = (bf16[512,1536]{1,0:T(8,128)(2,1)S(1)}, bf16[512,1536]{1,0:T(8,128)(2,1)}, u32[]{:S(2)}) copy-start(bf16[512,1536]{1,0:T(8,128)(2,1)} %all-gather.7.cloned.1.call-done) | copy-start | bytes 4718596
  33.0 4.0 %copy-start.3 = (bf16[1,8192,256]{2,1,0:T(8,128)(2,1)S(1)}, bf16[1,8192,256]{2,1,0:T(8,128)(2,1)}, u32[]{:S(2)}) copy-start(bf16[1,8192,256]{2,1,0:T(8,128)(2,1)} %v_ref.1) | copy-start | bytes 12582916
  36.1 2.2 copy-start.2
  62.2 0.7 copy-start.1
Sparse Core Ops, SparseCore 0:
  8.9 22.1 all-gather.6
  32.6 24.0 all-gather.8
  58.3 24.0 all-gather.10
  83.8 24.0 all-gather.12
  109.4 37.4 all-gather.14

commit v3 on v2

--- a/solution.py
+++ b/solution.py
@@ -138,10 +138,13 @@
     table,
     gain,
     w_out,
+    gate_part,
+    up_part,
+    down_part,
+    out_ref,
     gate,
     up,
     down,
-    out_ref,
     ctx_in,
     rows_g,
     rows_p,
@@ -165,6 +168,8 @@
     z_recv,
     end_send,
     end_recv,
+    weight_send,
+    weight_recv,
 ):
     tensor_count = lax.axis_size("tensor")
     tensor = lax.axis_index("tensor")
@@ -216,6 +221,22 @@
             remote(tab_g.at[step], tab_p.at[step], tab_send.at[1, step], tab_recv.at[1, step], partner),
         )
 
+    sibling = (tensor // 2) * 2 + (1 - tensor % 2)
+    across = (tensor + 2) % tensor_count
+    shards = ((gate_part, gate), (up_part, up), (down_part, down))
+
+    def weight_copy(number, leg):
+        shard, whole = shards[number]
+        slot = across if leg == 2 else tensor
+        source = whole.at[slot] if leg == 2 else shard
+        return remote(
+            source,
+            whole.at[slot],
+            weight_send.at[number, leg],
+            weight_recv.at[number, leg],
+            (expert, across if leg == 1 else sibling),
+        )
+
     def y_copy(step):
         return remote(out_y.at[step], in_y.at[step], y_send.at[step], y_recv.at[step], partner)
 
@@ -248,6 +269,10 @@
 
     for step in range(1, tensor_count):
         context_copy(step).start()
+    for number in range(3):
+        weight_copy(number, 1).start()
+    for number in range(3):
+        weight_copy(number, 0).start()
     mine = context[pl.ds(pl.multiple_of(tensor * quarter, quarter), quarter), :]
     total = base[...].astype(jnp.float32) + jnp.dot(
         mine, w_out[tensor], preferred_element_type=jnp.float32
@@ -282,14 +307,29 @@
         def _():
             z_copy(step).start()
 
+    for number in range(3):
+        shard, whole = shards[number]
+        whole[tensor] = shard[...]
+
+    def forward(step):
+        for copy in group_copies(step):
+            copy.wait_recv()
+        for copy in partner_copies(step):
+            copy.start()
+
+    for step in range(1, groups):
+        forward(step)
+        if step <= 3:
+            weight_copy(step - 1, 1).wait_recv()
+            weight_copy(step - 1, 2).start()
+    for number in range(min(groups - 1, 3), 3):
+        weight_copy(number, 1).wait_recv()
+        weight_copy(number, 2).start()
+    for number in range(3):
+        weight_copy(number, 0).wait_recv()
+        weight_copy(number, 2).wait_recv()
+
     def visit(step, carry):
-        @pl.when(step + 1 < groups)
-        def _():
-            for copy in group_copies(step + 1):
-                copy.wait_recv()
-            for copy in partner_copies(step + 1):
-                copy.start()
-
         for copy in partner_copies(step):
             copy.wait_recv()
         rows = jnp.concatenate([rows_g[step], rows_p[step]], axis=0)
@@ -328,6 +368,9 @@
         end_copy(step).wait_recv()
         end_copy(step).wait_send()
         context_copy(step).wait_send()
+    for number in range(3):
+        for leg in range(3):
+            weight_copy(number, leg).wait_send()
     for step in range(groups):
         for copy in partner_copies(step):
             copy.wait_send()
@@ -352,6 +395,9 @@
         in_specs=[pl.BlockSpec(memory_space=pltpu.VMEM)] * len(operands),
         out_specs=pl.BlockSpec(memory_space=pltpu.VMEM),
         scratch_shapes=[
+            pltpu.VMEM((tensor_count,) + gate.shape, jnp.bfloat16),
+            pltpu.VMEM((tensor_count,) + up.shape, jnp.bfloat16),
+            pltpu.VMEM((tensor_count,) + down.shape, jnp.bfloat16),
             pltpu.VMEM((tensor_count, quarter, context.shape[1]), jnp.bfloat16),
             pltpu.VMEM(block, jnp.bfloat16),
             pltpu.VMEM(block, jnp.bfloat16),
@@ -375,6 +421,8 @@
             dma((groups,)),
             dma((tensor_count,)),
             dma((tensor_count,)),
+            dma((3, 3)),
+            dma((3, 3)),
         ],
         compiler_params=pltpu.CompilerParams(
             collective_id=0, has_side_effects=True, vmem_limit_bytes=56 * 1024 * 1024
@@ -412,9 +460,6 @@
 
     full_rows = lax.all_gather(hidden_in, "tensor", axis=1, tiled=True)
     whole_out = lax.all_gather(w_out, "tensor", axis=0, tiled=False)
-    whole_gate = lax.all_gather(w_gate[0], "tensor", axis=0, tiled=False)
-    whole_up = lax.all_gather(w_up[0], "tensor", axis=0, tiled=False)
-    whole_down = lax.all_gather(w_down[0], "tensor", axis=0, tiled=False)
 
     my_ids = lax.dynamic_slice_in_dim(route_ids, tensor_index * quarter, quarter, 0)
     my_weights = lax.dynamic_slice_in_dim(route_weights, tensor_index * quarter, quarter, 0)
@@ -449,9 +494,9 @@
         table,
         moe_gain[None, :],
         whole_out,
-        whole_gate,
-        whole_up,
-        whole_down,
+        w_gate[0],
+        w_up[0],
+        w_down[0],
     )
 
 

time: 267 us -> 205 us (0.77)
  waiting for transfers between devices: 95.1 us -> 37.6 us
  local copies, waits for them, and re-layouts: 15.7 us -> 10.2 us
    all_gather x3 -> x0, waiting for transfers between devices: 35.9 us -> none  [the longest x1 21 us: local(): whole_down = lax.all_gather(w_down[0], 'tensor', axis=0, tiled=False)]
    all_gather x1, waiting for transfers between devices: 38.9 us -> 20.7 us  [local(): whole_out = lax.all_gather(w_out, 'tensor', axis=0, tiled=False)]
    pallas_call x1, Pallas kernels: 112 us -> 126 us  [tail(): pl.pallas_call(functools.partial(tail_kernel, groups), out_shape=jax.Shap...]
    pallas_call x1, Pallas kernels: 23.9 us -> 11.8 us  [attention(): pl.pallas_call(functools.partial(attention_kernel, heads, scale), grid_sp...]
    all_gather x2 -> x0, local copies, waits for them, and re-layouts: 9.09 us -> none  [the longest x1 4.56 us: local(): whole_up = lax.all_gather(w_up[0], 'tensor', axis=0, tiled=False)]
    unnamed x19 -> x23, local copies, waits for them, and re-layouts: 3.78 us -> 6.34 us
  transfers between devices with their start and end apart: 5 -> 2, of which waited for: 4 -> 2; matrix products, arithmetic and copies ran while one was open for 7% -> 5% of each run, Pallas kernels for 9% -> 6%
where the time goes in v3:
time: 205 us; the launch traced here: 204 us
  Pallas kernels  137 us (67%)
  waiting for transfers between devices  37.6 us (18%)
  between operations  14.9 us (7%)
  local copies, waits for them, and re-layouts  10.2 us (5%)
  other arithmetic  2.59 us (1%)
    pallas_call x1, Pallas kernels, tail(): pl.pallas_call(functools.partial(tail_kernel, groups), out_shape=jax.Shap...  126 us
    all_gather x1, waiting for transfers between devices, local(): whole_out = lax.all_gather(w_out, 'tensor', axis=0, tiled=False)  20.7 us
    all_gather x1, waiting for transfers between devices, local(): full_rows = lax.all_gather(hidden_in, 'tensor', axis=1, tiled=True)  15.6 us
    pallas_call x1, Pallas kernels, attention(): pl.pallas_call(functools.partial(attention_kernel, heads, scale), grid_sp...  11.8 us
    unnamed x23, local copies, waits for them, and re-layouts  6.34 us
  transfers between devices with their start and end apart: 2, of which 2 were waited for; matrix products, arithmetic and copies ran while one was open for 5% of the time, Pallas kernels for 6%

profile of v3, /device:TPU:1, one launch (start us, length us, event | category | flops | bytes accessed | tf_op | source)
XLA Modules:
  0.0 204.3 jit_solution(18171483389585303376)
XLA Ops:
  6.5 0.0 copy-start
  6.5 0.0 copy-start.5
  6.5 0.0 copy-start.6
  6.5 0.0 all-gather.4.cloned.1.call-start
  6.5 0.7 all-gather.4.cloned.1.call-update
  7.3 0.0 all-gather.6.cloned.1.call-start
  7.3 0.7 all-gather.6.cloned.1.call-update
  8.0 0.0 copy-start.8
  8.0 0.0 copy-start.7
  9.4 0.0 copy-done.5
  9.4 1.2 copy.21
  10.6 0.0 copy-done.6
  10.6 1.2 copy.22
  11.8 0.0 copy-done.8
  11.8 0.6 broadcast_in_dim.22.gain
  12.4 0.1 pad_add_fusion.info
  12.5 0.7 dynamic-slice_bitcast_fusion
  13.1 0.7 dynamic-slice_bitcast_fusion.1
  13.8 0.6 select_reduce_fusion.table
  14.4 0.0 copy-done.7
  14.4 0.0 copy-start.9
  14.4 1.1 constant_dynamic-slice_fusion.1
  15.5 15.6 %all-gather.4.cloned.1.call-done = bf16[512,1536]{1,0:T(8,128)(2,1)} async-done(((bf16[512,384]{1,0:T(8,128)(2,1)}), bf16[512,1536]{1,0:T(8,128)(2,1)}) %all-gather.4.cloned.1.call-update) | async-done | bytes 1572880 | tf_op jit(solution)/shard_map/all_gather | solution.py:461
  31.1 0.0 copy-start.4
  31.1 1.9 fusion
  33.0 0.0 copy-done.9
  33.0 0.0 copy-done.4
  33.0 0.0 copy-start.3
  33.0 0.6 convolution_convert_fusion.1
  33.7 0.8 constant_dynamic-slice_fusion.base
  34.5 0.0 copy-done
  34.5 0.0 copy-start.2
  34.5 0.9 fusion.3.q_ref
  35.5 0.0 copy-done.3
  35.5 1.4 copy-done.2
  36.9 11.8 %attention.1.context = bf16[512,384]{1,0:T(8,128)(2,1)S(1)} custom-call(s32[3]{0:T(128)S(1)} %pad_add_fusion.info, bf16[384,512]{1,0:T(8,128)(2,1)S(1)} %fusion.3.q_ref, bf16[512,128]{1,0:T(8,128)(2,1)S(1)} %get-tuple-element.6.nk_ref, bf16[512,128]{1,0:T(8,128)(2,1)S(1)} %get-tuple-element.5.nv_ref, bf16[1,8192,256]{2,1,0:T(8,128)(2,1)S(1)} %copy-done.2, ...), custom_call_target="tpu_custom_call" | custom-call | flops 6442450944 | bytes 4194304 | tf_op jit(solution)/shard_map/attention/pallas_call | solution.py:104
  48.7 0.0 copy-start.1
  48.8 0.7 copy-done.1
  49.5 20.7 %all-gather.6.cloned.1.call-done = bf16[1536,1536]{1,0:T(8,128)(2,1)} async-done(((bf16[384,1536]{1,0:T(8,128)(2,1)}), bf16[1536,1536]{1,0:T(8,128)(2,1)}) %all-gather.6.cloned.1.call-update) | async-done | bytes 4718608 | tf_op jit(solution)/shard_map/all_gather | solution.py:462
  70.1 125.5 %tail.1 = bf16[512,384]{1,0:T(8,128)(2,1)} custom-call(bf16[512,384]{1,0:T(8,128)(2,1)} %copy-done.1, bf16[128,1536]{1,0:T(8,128)(2,1)} %constant_dynamic-slice_fusion.base, f32[8,128]{1,0:T(8,128)} %select_reduce_fusion.table, f32[1,1536]{1,0:T(1,128)} %broadcast_in_dim.22.gain, bf16[4,384,1536]{2,1,0:T(8,128)(2,1)} %bitcast.12, ...), custom_call_target="tpu_custom_call" | custom-call | tf_op jit(solution)/shard_map/tail/pallas_call | solution.py:392
  195.7 1.8 copy.27
  (2 shorter events, 0.0 us)
Async XLA Ops:
  6.5 28.0 %copy-start = (bf16[1536,384]{1,0:T(8,128)(2,1)S(1)}, bf16[1536,384]{1,0:T(8,128)(2,1)}, u32[]{:S(2)}) copy-start(bf16[1536,384]{1,0:T(8,128)(2,1)} %param.22) | copy-start | bytes 3538948
  6.5 2.9 %copy-start.5 = (bf16[1,1536,192]{1,2,0:T(8,128)(2,1)S(1)}, bf16[1,1536,192]{1,2,0:T(8,128)(2,1)}, u32[]{:S(2)}) copy-start(bf16[1,1536,192]{1,2,0:T(8,128)(2,1)} %param.29) | copy-start | bytes 1769476
  6.5 4.1 %copy-start.6 = (bf16[1,1536,192]{1,2,0:T(8,128)(2,1)S(1)}, bf16[1,1536,192]{1,2,0:T(8,128)(2,1)}, u32[]{:S(2)}) copy-start(bf16[1,1536,192]{1,2,0:T(8,128)(2,1)} %param.30) | copy-start | bytes 1769476
  6.5 24.5 %all-gather.4.cloned.1.call-start = ((), (), s32[]{:S(2)}) async-start(), calls=%async_computation | async-start | bytes 1966080 | tf_op jit(solution)/shard_map/all_gather | solution.py:461
  7.3 62.9 %all-gather.6.cloned.1.call-start = ((), (), s32[]{:S(2)}) async-start(), calls=%async_computation.1 | async-start | bytes 5898240 | tf_op jit(solution)/shard_map/all_gather | solution.py:462
  8.0 3.8 %copy-start.8 = (f32[1536]{0:T(1024)S(1)}, f32[1536]{0:T(1024)}, u32[]{:S(2)}) copy-start(f32[1536]{0:T(1024)} %param.26) | copy-start | bytes 18436
  8.0 6.4 %copy-start.7 = (bf16[1536,256]{1,0:T(8,128)(2,1)S(1)}, bf16[1536,256]{1,0:T(8,128)(2,1)}, u32[]{:S(2)}) copy-start(bf16[1536,256]{1,0:T(8,128)(2,1)} %param.24) | copy-start | bytes 2359300
  14.4 18.6 %copy-start.9 = (f32[1536]{0:T(1024)S(1)}, f32[1536]{0:T(1024)}, u32[]{:S(2)}) copy-start(f32[1536]{0:T(1024)} %param.21) | copy-start | bytes 18436
  31.1 1.9 copy-start.4
  33.0 2.4 %copy-start.3 = (bf16[1,8192,256]{2,1,0:T(8,128)(2,1)S(1)}, bf16[1,8192,256]{2,1,0:T(8,128)(2,1)}, u32[]{:S(2)}) copy-start(bf16[1,8192,256]{2,1,0:T(8,128)(2,1)} %v_ref.1) | copy-start | bytes 12582916
  34.5 2.4 %copy-start.2 = (bf16[1,8192,256]{2,1,0:T(8,128)(2,1)S(1)}, bf16[1,8192,256]{2,1,0:T(8,128)(2,1)}, u32[]{:S(2)}) copy-start(bf16[1,8192,256]{2,1,0:T(8,128)(2,1)} %k_ref.1) | copy-start | bytes 12582916
  48.7 0.7 copy-start.1
Sparse Core Ops, SparseCore 0:
  8.9 22.1 all-gather.3
  32.6 37.4 all-gather.5

commit v4 on v3

--- a/solution.py
+++ b/solution.py
@@ -298,14 +298,9 @@
         row = jnp.sum(jnp.where(place == expert, tab, 0.0), axis=0, keepdims=True)
         return jnp.broadcast_to(row, (8, quarter)).T[:, :1]
 
-    def merge(step):
+    def joined(step, turn):
         y_copy(step).wait_recv()
-        joined = keep[step % 2] + in_y[step].astype(jnp.float32)
-        in_y[step] = joined.astype(jnp.bfloat16)
-
-        @pl.when(step > 0)
-        def _():
-            z_copy(step).start()
+        return keep[turn % 2] + in_y[step].astype(jnp.float32)
 
     for number in range(3):
         shard, whole = shards[number]
@@ -329,7 +324,8 @@
         weight_copy(number, 0).wait_recv()
         weight_copy(number, 2).wait_recv()
 
-    def visit(step, carry):
+    def visit(turn, carry):
+        step = (turn + 1) % groups
         for copy in partner_copies(step):
             copy.wait_recv()
         rows = jnp.concatenate([rows_g[step], rows_p[step]], axis=0)
@@ -342,18 +338,17 @@
             result = term if result is None else result + term
         out_y[step] = (result[quarter:] * column(tab_p[step])).astype(jnp.bfloat16)
         y_copy(step).start()
-        keep[step % 2] = result[:quarter] * column(tab_g[step])
-
-        @pl.when(step > 0)
+        keep[turn % 2] = result[:quarter] * column(tab_g[step])
+
+        @pl.when(turn > 0)
         def _():
-            merge(step - 1)
+            in_y[turn] = joined(turn, turn - 1).astype(jnp.bfloat16)
+            z_copy(turn).start()
 
         return carry
 
     lax.fori_loop(0, groups, visit, 0)
-    merge(groups - 1)
-
-    final = residual[...].astype(jnp.float32) + in_y[0].astype(jnp.float32)
+    final = residual[...].astype(jnp.float32) + joined(0, groups - 1)
     for step in range(1, groups):
         z_copy(step).wait_recv()
         final = final + in_z[step].astype(jnp.float32)

time: 205 us -> 196 us (0.956)
  Pallas kernels: 137 us -> 120 us
  waiting for transfers between devices: 37.6 us -> 46.6 us
    all_gather x1, waiting for transfers between devices: 20.7 us -> 29.6 us  [local(): whole_out = lax.all_gather(w_out, 'tensor', axis=0, tiled=False)]
    pallas_call x1, Pallas kernels: 11.8 us -> 2.91 us  [attention(): pl.pallas_call(functools.partial(attention_kernel, heads, scale), grid_sp...]
    pallas_call x1, Pallas kernels: 126 us -> 117 us  [tail(): pl.pallas_call(functools.partial(tail_kernel, groups), out_shape=jax.Shap...]
  transfers between devices with their start and end apart: 2 -> 2, of which waited for: 2 -> 2; matrix products, arithmetic and copies ran while one was open for 5% -> 5% of each run, Pallas kernels for 6% -> 1%
where the time goes in v4:
time: 196 us
  Pallas kernels  120 us (61%)
  waiting for transfers between devices  46.6 us (24%)
  between operations  14.9 us (8%)
  local copies, waits for them, and re-layouts  10.2 us (5%)
  other arithmetic  2.59 us (1%)
    pallas_call x1, Pallas kernels, tail(): pl.pallas_call(functools.partial(tail_kernel, groups), out_shape=jax.Shap...  117 us
    all_gather x1, waiting for transfers between devices, local(): whole_out = lax.all_gather(w_out, 'tensor', axis=0, tiled=False)  29.6 us
    all_gather x1, waiting for transfers between devices, local(): full_rows = lax.all_gather(hidden_in, 'tensor', axis=1, tiled=True)  15.6 us
    unnamed x23, local copies, waits for them, and re-layouts  6.34 us
  transfers between devices with their start and end apart: 2, of which 2 were waited for; matrix products, arithmetic and copies ran while one was open for 5% of the time, Pallas kernels for 1%

profile of v4, /device:TPU:1, one launch (start us, length us, event | category | flops | bytes accessed | tf_op | source)
XLA Modules:
  0.0 195.9 jit_solution(3242738756949971234)
XLA Ops:
  6.5 0.0 copy-start
  6.5 0.0 copy-start.5
  6.5 0.0 copy-start.6
  6.5 0.0 all-gather.4.cloned.1.call-start
  6.5 0.7 all-gather.4.cloned.1.call-update
  7.3 0.0 all-gather.6.cloned.1.call-start
  7.3 0.7 all-gather.6.cloned.1.call-update
  8.0 0.0 copy-start.8
  8.0 0.0 copy-start.7
  9.4 0.0 copy-done.5
  9.4 1.2 copy.21
  10.6 0.0 copy-done.6
  10.6 1.2 copy.22
  11.8 0.0 copy-done.8
  11.8 0.6 broadcast_in_dim.22.gain
  12.4 0.1 pad_add_fusion.info
  12.5 0.7 dynamic-slice_bitcast_fusion
  13.1 0.7 dynamic-slice_bitcast_fusion.1
  13.8 0.6 select_reduce_fusion.table
  14.4 0.0 copy-done.7
  14.4 0.0 copy-start.9
  14.4 1.1 constant_dynamic-slice_fusion.1
  15.5 15.6 %all-gather.4.cloned.1.call-done = bf16[512,1536]{1,0:T(8,128)(2,1)} async-done(((bf16[512,384]{1,0:T(8,128)(2,1)}), bf16[512,1536]{1,0:T(8,128)(2,1)}) %all-gather.4.cloned.1.call-update) | async-done | bytes 1572880 | tf_op jit(solution)/shard_map/all_gather | solution.py:456
  31.1 0.0 copy-start.4
  31.1 1.9 fusion
  33.0 0.0 copy-done.9
  33.0 0.0 copy-done.4
  33.0 0.0 copy-start.3
  33.0 0.6 convolution_convert_fusion.1
  33.7 0.8 constant_dynamic-slice_fusion.base
  34.5 0.0 copy-done
  34.5 0.0 copy-start.2
  34.5 0.9 fusion.3.q_ref
  35.5 0.0 copy-done.3
  35.5 1.4 copy-done.2
  36.9 2.9 %attention.1.context = bf16[512,384]{1,0:T(8,128)(2,1)S(1)} custom-call(s32[3]{0:T(128)S(1)} %pad_add_fusion.info, bf16[384,512]{1,0:T(8,128)(2,1)S(1)} %fusion.3.q_ref, bf16[512,128]{1,0:T(8,128)(2,1)S(1)} %get-tuple-element.6.nk_ref, bf16[512,128]{1,0:T(8,128)(2,1)S(1)} %get-tuple-element.5.nv_ref, bf16[1,8192,256]{2,1,0:T(8,128)(2,1)S(1)} %copy-done.2, ...), custom_call_target="tpu_custom_call" | custom-call | flops 6442450944 | bytes 4194304 | tf_op jit(solution)/shard_map/attention/pallas_call | solution.py:104
  39.8 0.0 copy-start.1
  39.8 0.7 copy-done.1
  40.6 29.6 %all-gather.6.cloned.1.call-done = bf16[1536,1536]{1,0:T(8,128)(2,1)} async-done(((bf16[384,1536]{1,0:T(8,128)(2,1)}), bf16[1536,1536]{1,0:T(8,128)(2,1)}) %all-gather.6.cloned.1.call-update) | async-done | bytes 4718608 | tf_op jit(solution)/shard_map/all_gather | solution.py:457
  70.1 117.1 %tail.1 = bf16[512,384]{1,0:T(8,128)(2,1)} custom-call(bf16[512,384]{1,0:T(8,128)(2,1)} %copy-done.1, bf16[128,1536]{1,0:T(8,128)(2,1)} %constant_dynamic-slice_fusion.base, f32[8,128]{1,0:T(8,128)} %select_reduce_fusion.table, f32[1,1536]{1,0:T(1,128)} %broadcast_in_dim.22.gain, bf16[4,384,1536]{2,1,0:T(8,128)(2,1)} %bitcast.12, ...), custom_call_target="tpu_custom_call" | custom-call | tf_op jit(solution)/shard_map/tail/pallas_call | solution.py:387
  187.3 1.8 copy.27
  (2 shorter events, 0.0 us)
Async XLA Ops:
  6.5 28.0 %copy-start = (bf16[1536,384]{1,0:T(8,128)(2,1)S(1)}, bf16[1536,384]{1,0:T(8,128)(2,1)}, u32[]{:S(2)}) copy-start(bf16[1536,384]{1,0:T(8,128)(2,1)} %param.22) | copy-start | bytes 3538948
  6.5 2.9 %copy-start.5 = (bf16[1,1536,192]{1,2,0:T(8,128)(2,1)S(1)}, bf16[1,1536,192]{1,2,0:T(8,128)(2,1)}, u32[]{:S(2)}) copy-start(bf16[1,1536,192]{1,2,0:T(8,128)(2,1)} %param.29) | copy-start | bytes 1769476
  6.5 4.1 %copy-start.6 = (bf16[1,1536,192]{1,2,0:T(8,128)(2,1)S(1)}, bf16[1,1536,192]{1,2,0:T(8,128)(2,1)}, u32[]{:S(2)}) copy-start(bf16[1,1536,192]{1,2,0:T(8,128)(2,1)} %param.30) | copy-start | bytes 1769476
  6.5 24.5 %all-gather.4.cloned.1.call-start = ((), (), s32[]{:S(2)}) async-start(), calls=%async_computation | async-start | bytes 1966080 | tf_op jit(solution)/shard_map/all_gather | solution.py:456
  7.3 62.9 %all-gather.6.cloned.1.call-start = ((), (), s32[]{:S(2)}) async-start(), calls=%async_computation.1 | async-start | bytes 5898240 | tf_op jit(solution)/shard_map/all_gather | solution.py:457
  8.0 3.8 %copy-start.8 = (f32[1536]{0:T(1024)S(1)}, f32[1536]{0:T(1024)}, u32[]{:S(2)}) copy-start(f32[1536]{0:T(1024)} %param.26) | copy-start | bytes 18436
  8.0 6.4 %copy-start.7 = (bf16[1536,256]{1,0:T(8,128)(2,1)S(1)}, bf16[1536,256]{1,0:T(8,128)(2,1)}, u32[]{:S(2)}) copy-start(bf16[1536,256]{1,0:T(8,128)(2,1)} %param.24) | copy-start | bytes 2359300
  14.4 18.6 %copy-start.9 = (f32[1536]{0:T(1024)S(1)}, f32[1536]{0:T(1024)}, u32[]{:S(2)}) copy-start(f32[1536]{0:T(1024)} %param.21) | copy-start | bytes 18436
  31.1 1.9 copy-start.4
  33.0 2.4 %copy-start.3 = (bf16[1,8192,256]{2,1,0:T(8,128)(2,1)S(1)}, bf16[1,8192,256]{2,1,0:T(8,128)(2,1)}, u32[]{:S(2)}) copy-start(bf16[1,8192,256]{2,1,0:T(8,128)(2,1)} %v_ref.1) | copy-start | bytes 12582916
  34.5 2.4 %copy-start.2 = (bf16[1,8192,256]{2,1,0:T(8,128)(2,1)S(1)}, bf16[1,8192,256]{2,1,0:T(8,128)(2,1)}, u32[]{:S(2)}) copy-start(bf16[1,8192,256]{2,1,0:T(8,128)(2,1)} %k_ref.1) | copy-start | bytes 12582916
  39.8 0.7 copy-start.1
Sparse Core Ops, SparseCore 0:
  8.9 22.1 all-gather.3
  32.6 37.4 all-gather.5
